TPU v7x, 512 devices: a whole 4x8x8 slice. The times are simulated.
512 devices in a mesh: dp: 128 (over z, y, core), out: 4 (over x).
Axes of the slice: x: 4, y: 8, z: 8, core: 2. Of those that a mesh axis runs over, the one named last changes fastest.
Arguments:
- points: bfloat16 [196608, 440], P('dp'), may hold values from -6 to 6
- weights: float32 [256, 196608], P('out', 'dp'), may hold values from -0.6 to 0.6
- targets: float32 [256, 196608], P('out', 'dp'), may hold values from -6 to 6
- fitted: float32 [256, 196608], P('out', 'dp'), may hold values from -6 to 6
- preconditioner: float32 [2, 1024, 1024], P(None, 'dp'), may hold values from -2 to 3
- owners: int32 [2], replicated, may hold values from 0 to 127
- block_index: int32 [2, 1024], replicated, may hold values from 0 to 1535, as said below
Outputs:
- new_weights: float32 [256, 196608], P('out', 'dp')
- new_fitted: float32 [256, 196608], P('out', 'dp')
Inputs may be any that keep to these rules, and one draw needn't show every extreme that they name: `block_index`: within one step the 1024 point numbers are distinct.
All inputs are finite; a program needn't handle non-finite values.
Results may differ from a plain program's by a relative error of at most 0.0003.
Values may be sent and summed in bfloat16 or wider, within the bound.
No kernel may reach another device: no remote copies, remote signals or barrier semaphores. Data moves between devices by JAX's collectives and lax.ppermute only.
A program may use at most 64 MiB of HBM per device.

v0:
```python
import jax
import jax.numpy as jnp
from jax import lax
from jax.sharding import PartitionSpec as P

LAMBDA = 0.5


def broadcast(block, axis, holder):
    block = jnp.where(lax.axis_index(axis) == holder, block, jnp.zeros_like(block))
    return lax.psum(block, axis)


def local(points, weights, targets, fitted, preconditioner, owners, block_index):
    gamma = 2.0 / points.shape[1]
    rank = lax.axis_index("dp")
    wide_points = points.astype(jnp.float32)
    point_norm = jnp.sum(wide_points * wide_points, axis=1)
    for step in range(preconditioner.shape[0]):
        owner = owners[step]
        index = block_index[step]
        is_owner = rank == owner
        candidate = points[index]
        block = broadcast(candidate, "dp", owner)
        wide_block = block.astype(jnp.float32)
        block_norm = jnp.sum(wide_block * wide_block, axis=1)
        cross = jnp.dot(points, block.T, preferred_element_type=jnp.float32)
        kern = jnp.exp(-gamma * (point_norm[:, None] + block_norm[None, :] - 2.0 * cross))
        partial_sum = jnp.dot(weights, kern, precision=lax.Precision.HIGHEST)
        own_term = jnp.where(is_owner, LAMBDA * weights[:, index] - targets[:, index], 0.0)
        grad = lax.psum(partial_sum + own_term, "dp")
        my_rows = jnp.dot(grad, preconditioner[step].T, precision=lax.Precision.HIGHEST)
        delta = lax.all_gather(my_rows, "dp", axis=1, tiled=True)
        fitted = fitted - jnp.dot(delta, kern.T, precision=lax.Precision.HIGHEST)
        weights = weights.at[:, index].add(jnp.where(is_owner, -delta, 0.0))
    return (weights, fitted)


def solution(mesh):
    return jax.shard_map(
        local,
        mesh=mesh,
        in_specs=(
            P("dp", None),
            P("out", "dp"),
            P("out", "dp"),
            P("out", "dp"),
            P(None, "dp", None),
            P(),
            P(),
        ),
        out_specs=(P("out", "dp"), P("out", "dp")),
        check_vma=False,
    )
```

profile of v0, /device:TPU:1, one launch (start us, length us, event | category | flops | bytes accessed | tf_op | source)
XLA Modules:
  0.0 762.3 jit_solution(3374506020029739393)
XLA Ops:
  7.2 0.0 all-reduce.9.cloned.1.call-start
  7.2 0.8 compare_select_fusion
  8.0 1.7 copy.16
  9.7 4.0 gather_fusion
  13.7 0.0 copy-start.8
  13.7 0.0 copy-start.5
  13.7 5.1 gather_fusion.3
  18.8 0.0 copy-start.2
  18.8 0.0 copy-done.8
  18.8 0.6 fusion.23
  20.7 1.5 broadcast_select_fusion
  22.2 0.0 copy-start.1
  22.2 0.0 all-reduce.9.cloned.1.call-update
  22.2 0.0 all-reduce.5.cloned.1.call-start
  22.3 0.0 copy-done.5
  22.3 0.3 copy.18
  22.5 4.0 gather_fusion.2
  26.5 2.8 gather_fusion.5
  29.3 0.0 copy-done.2
  29.4 0.3 copy.19
  29.6 4.0 gather_fusion.1
  33.6 0.0 copy-done.1
  33.6 0.3 multiply_reduce_fusion
  33.9 194.3 %all-reduce.9.cloned.1.call-done = (bf16[1024,440]{1,0:T(8,128)(2,1)}, bf16[1024,440]{1,0:T(8,128)(2,1)}) async-done(((bf16[1024,440]{1,0:T(8,128)(2,1)}, bf16[1024,440]{1,0:T(8,128)(2,1)}), (bf16[1024,440]{1,0:T(8,128)(2,1)}, bf16[1024,440]{1,0:T(8,128)(2,1)})) %all-reduce.9.cloned.1.call-update) | async-done | bytes 1802256 | tf_op jit(solution)/shard_map/psum | solution.py:11
  228.2 1.5 multiply_reduce_fusion.2
  229.7 0.0 copy-start.3
  229.7 0.0 copy-start.4
  229.7 3.3 fusion.3
  233.1 0.0 copy-start
  233.1 2.7 copy-done
  235.7 0.0 copy-done.3
  235.7 0.0 copy-done.4
  235.7 5.9 fusion.4
  241.6 0.0 all-reduce.5.cloned.1.call-update
  241.7 0.2 all-reduce.7.cloned.1.call-start
  241.9 1.5 multiply_reduce_fusion.1
  243.4 0.0 copy-start.7
  243.4 5.9 fusion.1
  249.3 181.2 %all-reduce.5.cloned.1.call-done = f32[64,1024]{0,1:T(8,128)} async-done(((f32[64,1024]{0,1:T(8,128)}), f32[64,1024]{0,1:T(8,128)}) %all-reduce.5.cloned.1.call-update) | async-done | bytes 262160 | tf_op jit(solution)/shard_map/psum | solution.py:31
  430.5 0.0 copy-done.7
  430.5 1.4 fusion.19
  431.9 51.8 %all_gather.6 = f32[64,1024]{0,1:T(8,128)S(1)} all-gather(f32[64,8]{0,1:T(8,128)S(1)} %fusion.19), channel_id=1, replica_groups=mesh['dp'=128,'out'=4] {'dp'}, dimensions={1}, use_global_device_ids=true | all-gather | bytes 264192 | tf_op jit(solution)/shard_map/all_gather | solution.py:33
  483.7 0.0 copy-start.6
  483.7 6.4 scatter_custom_fusion
  490.1 2.8 gather_fusion.4
  492.9 8.1 %convolution_add_fusion = f32[64,1024]{0,1:T(8,128)} fusion(f32[64,1536]{0,1:T(8,128)S(1)} %scatter_custom_fusion, f32[1536,1024]{0,1:T(8,128)} %fusion.1, f32[1024,64]{1,0:T(8,128)S(1)} %gather_fusion.5, f32[1024,64]{1,0:T(8,128)S(1)} %gather_fusion.4, pred[]{:T(512)S(6)} %eq.9), kind=kOutput, calls=%fused_computation.19 | convolution fusion | flops 1208221696 | bytes 7471105 | tf_op jit(solution)/shard_map/dot_general | solution.py:29
  501.0 0.0 all-reduce.7.cloned.1.call-update
  501.0 0.0 copy-done.6
  501.0 5.9 convolution_subtract_fusion.1
  506.9 180.6 %all-reduce.7.cloned.1.call-done = f32[64,1024]{0,1:T(8,128)} async-done(((f32[64,1024]{0,1:T(8,128)}), f32[64,1024]{0,1:T(8,128)}) %all-reduce.7.cloned.1.call-update) | async-done | bytes 262160 | tf_op jit(solution)/shard_map/psum | solution.py:31
  687.5 1.4 fusion.17
  688.9 52.0 %all_gather.7 = f32[64,1024]{0,1:T(8,128)S(1)} all-gather(f32[64,8]{0,1:T(8,128)S(1)} %fusion.17), channel_id=1, replica_groups=mesh['dp'=128,'out'=4] {'dp'}, dimensions={1}, use_global_device_ids=true | all-gather | bytes 264192 | tf_op jit(solution)/shard_map/all_gather | solution.py:33
  741.0 6.4 scatter_custom_fusion.1
  747.3 7.4 convolution_subtract_fusion
  754.8 1.0 copy.22
  (2 shorter events, 0.0 us)
Async XLA Ops:
  7.2 221.0 %all-reduce.9.cloned.1.call-start = ((), (), s32[]{:S(2)}) async-start(), calls=%async_computation.2 | async-start | bytes 4194304 | tf_op jit(solution)/shard_map/psum | solution.py:11
  13.7 5.1 copy-start.8
  13.7 8.6 %copy-start.5 = (f32[64,1536]{1,0:T(8,128)S(1)}, f32[64,1536]{1,0:T(8,128)}, u32[]{:S(2)}) copy-start(f32[64,1536]{1,0:T(8,128)} %param.9) | copy-start | bytes 1179652
  18.8 10.6 %copy-start.2 = (f32[64,1536]{1,0:T(8,128)S(1)}, f32[64,1536]{1,0:T(8,128)}, u32[]{:S(2)}) copy-start(f32[64,1536]{1,0:T(8,128)} %param.8) | copy-start | bytes 1179652
  22.2 11.4 %copy-start.1 = (bf16[1536,440]{0,1:T(8,128)(2,1)S(1)}, bf16[1536,440]{0,1:T(8,128)(2,1)}, u32[]{:S(2)}) copy-start(bf16[1536,440]{0,1:T(8,128)(2,1)} %param.7) | copy-start | bytes 4055044
  22.2 408.3 %all-reduce.5.cloned.1.call-start = ((), (), s32[]{:S(2)}) async-start(), calls=%async_computation | async-start | bytes 1048576 | tf_op jit(solution)/shard_map/psum | solution.py:31
  229.7 6.0 copy-start.3
  229.7 6.0 copy-start.4
  233.1 2.7 copy-start
  241.7 445.9 %all-reduce.7.cloned.1.call-start = ((), (), s32[]{:S(2)}) async-start(), calls=%async_computation.1 | async-start | bytes 1048576 | tf_op jit(solution)/shard_map/psum | solution.py:31
  243.4 187.1 %copy-start.7 = (f32[2,8,1024]{2,1,0:T(8,128)S(1)}, f32[2,8,1024]{2,1,0:T(8,128)}, u32[]{:S(2)}) copy-start(f32[2,8,1024]{2,1,0:T(8,128)} %param.11) | copy-start | bytes 196612
  483.7 17.3 %copy-start.6 = (f32[64,1536]{1,0:T(8,128)S(1)}, f32[64,1536]{1,0:T(8,128)}, u32[]{:S(2)}) copy-start(f32[64,1536]{1,0:T(8,128)} %param.10) | copy-start | bytes 1179652
Sparse Core Ops, SparseCore 0:
  22.3 205.8 all-reduce.8
  241.8 188.6 all-reduce.4
  501.1 186.3 all-reduce.6
where the time goes:
time: 763 us; the launch traced here: 762 us
  waiting for transfers between devices  556 us (73%)
  blocking collectives  104 us (14%)
  matrix products  39.4 us (5%)
  local copies, waits for them, and re-layouts  29.1 us (4%)
  other arithmetic  18.4 us (2%)
  between operations  15.2 us (2%)
    psum x2, waiting for transfers between devices, local(): grad = lax.psum(partial_sum + own_term, 'dp')  362 us
    psum x1, waiting for transfers between devices, broadcast(): return lax.psum(block, axis)  194 us
    all_gather x2, blocking collectives, local(): delta = lax.all_gather(my_rows, 'dp', axis=1, tiled=True)  104 us
  transfers between devices with their start and end apart: 3, of which 3 were waited for; matrix products, arithmetic and copies ran while one was open for 3% of the time, Pallas kernels for 0%

commit v1 on v0

v1 whole, which is shorter than its diff:
```python
import functools

import jax
import jax.numpy as jnp
from jax import lax
from jax.experimental import pallas as pl
from jax.experimental.pallas import tpu as pltpu
from jax.sharding import Mesh, PartitionSpec as P

LAMBDA = 0.5
GRID = (8, 8, 2)
ZY = ("z", "y")
DP = ("z", "y", "c")
FEATURE_ROWS = 512
LANES = 128
CHUNK = 256
VMEM_BYTES = 48 * 1024 * 1024
BF16 = jnp.bfloat16
F32 = jnp.float32
TRANSPOSED = (((1,), (1,)), ((), ()))
FIRST_DIMS = (((0,), (0,)), ((), ()))

CORE, LINE, OWNS, SAME_OWNER = 0, 1, 2, 4


def params():
    return pltpu.CompilerParams(vmem_limit_bytes=VMEM_BYTES)


def exchange(value):
    return lax.ppermute(value, "c", [(0, 1), (1, 0)])


def all_to_all(value, axes):
    return lax.all_to_all(value, axes, 0, 0, tiled=True)


def two_parts(value):
    high = value.astype(BF16)
    return high, (value - high.astype(F32)).astype(BF16)


def three_parts(value):
    high = value.astype(BF16)
    rest = value - high.astype(F32)
    middle = rest.astype(BF16)
    return high, middle, (rest - middle.astype(F32)).astype(BF16)


def dot(left, right, dims=(((1,), (0,)), ((), ()))):
    return lax.dot_general(left, right, dims, preferred_element_type=F32)


def one_hot(count, numbers):
    rows = lax.broadcasted_iota(jnp.int32, (count, numbers.shape[1]), 0)
    return jnp.where(rows == numbers, 1.0, 0.0).astype(BF16)


def index_tile(index_ref, step, line, kind):
    return index_ref[step, pl.ds(2 * line + kind, 1), :]


def pick_kernel(info, points_ref, index_ref, keep_ref, send_ref):
    count, features = points_ref.shape
    steps = index_ref.shape[0]
    core, line = info[CORE], info[LINE]
    numbers = [
        index_tile(index_ref, step, line, kind)
        for kind in (core, 1 - core)
        for step in range(steps)
    ]
    picked = dot(points_ref[...], one_hot(count, jnp.concatenate(numbers, axis=1)), FIRST_DIMS)
    empty = jnp.zeros((FEATURE_ROWS - features, picked.shape[1]), F32)
    picked = jnp.concatenate([picked, empty], axis=0).astype(BF16)
    for place, ref in enumerate((keep_ref, send_ref)):
        for step in range(steps):
            at = (place * steps + step) * LANES
            ref[step] = picked[:, at : at + LANES]


def pick_blocks(info, points, index):
    steps = index.shape[0]
    shape = jax.ShapeDtypeStruct((steps, FEATURE_ROWS, LANES), BF16)
    return pl.pallas_call(
        pick_kernel,
        grid_spec=pltpu.PrefetchScalarGridSpec(
            num_scalar_prefetch=1,
            grid=(),
            in_specs=[pl.BlockSpec(memory_space=pltpu.VMEM)] * 2,
            out_specs=[pl.BlockSpec(memory_space=pltpu.VMEM)] * 2,
        ),
        out_shape=[shape, shape],
        compiler_params=params(),
        name="pick_blocks",
    )(info, points, index)


def kernel_kernel(
    foreign,
    info,
    points_ref,
    weights_ref,
    targets_ref,
    index_ref,
    blocks_ref,
    grad_ref,
    high_ref,
    low_ref,
    parts,
    norms,
):
    count, features = points_ref.shape
    outs = weights_ref.shape[0]
    gamma = 2.0 / features
    step, pair = pl.program_id(0), pl.program_id(1)

    @pl.when((step == 0) & (pair == 0))
    def _():
        high, low = two_parts(weights_ref[...])
        parts[:outs, :] = high
        parts[outs:, :] = low
        for at in range(0, count, CHUNK):
            wide = points_ref[at : at + CHUNK, :].astype(F32)
            norms[at : at + CHUNK, :] = gamma * jnp.sum(wide * wide, axis=1, keepdims=True)

    block = jnp.concatenate([blocks_ref[0], blocks_ref[1]], axis=1)
    wide = block.astype(F32)
    block_norm = gamma * jnp.sum(wide * wide, axis=0, keepdims=True)
    grad = jnp.zeros((outs, 2 * LANES), F32)
    for at in range(0, count, CHUNK):
        rows = slice(at, at + CHUNK)
        cross = dot(points_ref[rows, :], block[:features, :])
        kern = jnp.exp((2.0 * gamma) * cross - (norms[rows, :] + block_norm))
        high, low = two_parts(kern)
        high_ref[0, 0, rows, :] = high
        low_ref[0, 0, rows, :] = low
        both = dot(parts[:, rows], high)
        grad = grad + (both[:outs] + both[outs:] + dot(parts[:outs, rows], low))
    grad_ref[0, 0] = grad

    @pl.when(info[OWNS + step] == 1)
    def _():
        kind = info[CORE] ^ foreign
        numbers = [index_tile(index_ref, step, 2 * pair + k, kind) for k in range(2)]
        pick = one_hot(count, jnp.concatenate(numbers, axis=1))
        own = LAMBDA * weights_ref[...] - targets_ref[...]
        terms = [dot(part, pick) for part in three_parts(own)]
        grad_ref[0, 0] += terms[0] + (terms[1] + terms[2])


def kernel_and_gradient(foreign, info, points, weights, targets, index, blocks):
    count = points.shape[0]
    outs = weights.shape[0]
    steps = index.shape[0]
    pairs = blocks.shape[0] // 2
    whole = pl.BlockSpec(memory_space=pltpu.VMEM)
    kern_shape = jax.ShapeDtypeStruct((steps, pairs, count, 2 * LANES), BF16)
    kern_spec = pl.BlockSpec((1, 1, count, 2 * LANES), lambda s, p, info: (s, p, 0, 0))
    return pl.pallas_call(
        functools.partial(kernel_kernel, foreign),
        grid_spec=pltpu.PrefetchScalarGridSpec(
            num_scalar_prefetch=1,
            grid=(steps, pairs),
            in_specs=[whole] * 4
            + [pl.BlockSpec((2, FEATURE_ROWS, LANES), lambda s, p, info: (p, s, 0))],
            out_specs=[
                pl.BlockSpec((1, 1, outs, 2 * LANES), lambda s, p, info: (s, p, 0, 0)),
                kern_spec,
                kern_spec,
            ],
            scratch_shapes=[
                pltpu.VMEM((2 * outs, count), BF16),
                pltpu.VMEM((count, 1), F32),
            ],
        ),
        out_shape=[
            jax.ShapeDtypeStruct((steps, pairs, outs, 2 * LANES), F32),
            kern_shape,
            kern_shape,
        ],
        compiler_params=params(),
        name="kernel_and_gradient",
    )(info, points, weights, targets, index, blocks)


def between_kernel(features, info, index_ref, own_ref, other_ref, out_ref):
    lines = own_ref.shape[0]
    gamma = 2.0 / features
    core = info[CORE]

    def tile(step, line, kind):
        at = step * FEATURE_ROWS
        rows = slice(at, at + FEATURE_ROWS)
        return jnp.where(core == kind, own_ref[line, rows, :], other_ref[line, rows, :])

    places = [(line, kind) for line in range(lines) for kind in range(2)]
    second = jnp.concatenate([tile(1, *place) for place in places], axis=1)
    wide = second.astype(F32)
    second_norm = gamma * jnp.sum(wide * wide, axis=0, keepdims=True)
    second_index = jnp.concatenate(
        [index_ref[1, n : n + 1, :] for n in range(len(places))], axis=1
    )
    extra = jnp.where(info[SAME_OWNER] == 1, LAMBDA, 0.0)
    for n, place in enumerate(places):
        first = tile(0, *place)
        wide = first.astype(F32)
        square = jnp.sum(wide * wide, axis=0, keepdims=True)
        first_norm = gamma * jnp.transpose(jnp.broadcast_to(square, (LANES, LANES)))[:, :1]
        first_index = jnp.transpose(
            jnp.broadcast_to(index_ref[0, n : n + 1, :].astype(F32), (LANES, LANES))
        )[:, :1].astype(jnp.int32)
        cross = dot(first, second, FIRST_DIMS)
        kern = jnp.exp((2.0 * gamma) * cross - (first_norm + second_norm))
        out_ref[n * LANES : (n + 1) * LANES, :] = kern + jnp.where(
            first_index == second_index, extra, 0.0
        )


def between_blocks(features, info, index, own, other):
    block = index.shape[1] * LANES
    whole = pl.BlockSpec(memory_space=pltpu.VMEM)
    return pl.pallas_call(
        functools.partial(between_kernel, features),
        grid_spec=pltpu.PrefetchScalarGridSpec(
            num_scalar_prefetch=1, grid=(), in_specs=[whole] * 3, out_specs=whole
        ),
        out_shape=jax.ShapeDtypeStruct((block, block), F32),
        compiler_params=params(),
        cost_estimate=pl.CostEstimate(
            flops=2 * block * block * FEATURE_ROWS,
            bytes_accessed=4 * block * block,
            transcendentals=block * block,
        ),
        name="between_blocks",
    )(info, index, own, other)


def chain_kernel(info, mine_ref, theirs_ref, given_ref, between_ref, out_ref, grads, sums):
    step, part = pl.program_id(0), pl.program_id(1)
    parts = pl.num_programs(1)
    tiles = out_ref.shape[1]
    lines = tiles // 2
    core = info[CORE]

    @pl.when((step == 0) & (part == 0))
    def _():
        half = 2 * lines
        own = mine_ref[:half, :] + theirs_ref[half:, :]
        other = mine_ref[half:, :] + theirs_ref[:half, :]
        for s in range(2):
            for line in range(lines):
                at = slice(s * lines + line, s * lines + line + 1)
                for kind in range(2):
                    lanes = slice((2 * line + kind) * LANES, (2 * line + kind + 1) * LANES)
                    grads[s : s + 1, lanes] = jnp.where(core == kind, own[at, :], other[at, :])
        sums[...] = jnp.zeros_like(sums)

    @pl.when((step == 1) & (part == 0))
    def _():
        total = jnp.sum(sums[...], axis=0, keepdims=True)
        grads[1:2, :] = grads[1:2, :] - total

    grad = grads[pl.ds(step, 1), :]
    given = given_ref[...]
    given = given.reshape(-1, given.shape[-1])
    delta = jnp.sum(given * grad, axis=1, keepdims=True)

    @pl.when(step == 0)
    def _():
        product = delta * between_ref[...]
        sums[...] += jnp.sum(product.reshape(-1, *sums.shape), axis=0)

    diagonal = lax.broadcasted_iota(jnp.int32, (LANES, LANES), 0) == lax.broadcasted_iota(
        jnp.int32, (LANES, LANES), 1
    )
    rows = given.shape[0]
    for n in range(rows // LANES):
        column = delta[n * LANES : (n + 1) * LANES, :]
        row = jnp.sum(jnp.where(diagonal, column, 0.0), axis=0, keepdims=True)
        out_ref[pl.ds(step, 1), pl.ds(part * (rows // LANES) + n, 1), :] = row[None]


def run_chain(info, mine, theirs, given, between):
    devices, steps, rows, block = given.shape
    parts = 4
    share = devices // parts
    whole = pl.BlockSpec(memory_space=pltpu.VMEM)
    return pl.pallas_call(
        chain_kernel,
        grid_spec=pltpu.PrefetchScalarGridSpec(
            num_scalar_prefetch=1,
            grid=(steps, parts),
            in_specs=[
                whole,
                whole,
                pl.BlockSpec((share, 1, rows, block), lambda s, p, info: (p, s, 0, 0)),
                pl.BlockSpec(
                    (share * rows, block),
                    lambda s, p, info: (jnp.where(s == 0, p, parts - 1), 0),
                ),
            ],
            out_specs=whole,
            scratch_shapes=[pltpu.VMEM((steps, block), F32), pltpu.VMEM((8, block), F32)],
        ),
        out_shape=jax.ShapeDtypeStruct((steps, block // LANES, LANES), F32),
        compiler_params=params(),
        name="run_chain",
    )(info, mine, theirs, given, between)


def update_kernel(
    foreign,
    info,
    delta_ref,
    index_ref,
    weights_ref,
    fitted_ref,
    own_high,
    own_low,
    other_high,
    other_low,
    new_weights_ref,
    new_fitted_ref,
):
    pair = pl.program_id(0)
    core = info[CORE]
    step = core ^ foreign
    outs, count = weights_ref.shape

    @pl.when(pair == 0)
    def _():
        new_weights_ref[...] = weights_ref[...]
        new_fitted_ref[...] = fitted_ref[...]

    def tile(kind):
        tiles = [
            delta_ref[:, pl.ds(2 * (2 * pair + k) + kind, 1), :].reshape(outs, LANES)
            for k in range(2)
        ]
        return jnp.concatenate(tiles, axis=1)

    for high_ref, low_ref, kind in (
        (own_high, own_low, core),
        (other_high, other_low, 1 - core),
    ):
        delta = tile(kind)
        high, low = two_parts(delta)
        both = jnp.concatenate([high, low], axis=0)
        for at in range(0, count, CHUNK):
            rows = slice(at, at + CHUNK)
            change = dot(both, high_ref[0, 0, rows, :], TRANSPOSED)
            small = dot(high, low_ref[0, 0, rows, :], TRANSPOSED)
            new_fitted_ref[:, rows] -= change[:outs] + (change[outs:] + small)

        @pl.when(info[OWNS + step] == 1)
        def _():
            numbers = [index_tile(index_ref, step, 2 * pair + k, kind) for k in range(2)]
            pick = one_hot(count, jnp.concatenate(numbers, axis=1))
            terms = [dot(part, pick, TRANSPOSED) for part in three_parts(delta)]
            new_weights_ref[...] -= terms[0] + (terms[1] + terms[2])


def update(foreign, info, delta, index, weights, fitted, own, other):
    outs, count = weights.shape
    pairs = own[0].shape[1]
    whole = pl.BlockSpec(memory_space=pltpu.VMEM)
    kern_spec = pl.BlockSpec(
        (1, 1, count, 2 * LANES), lambda p, info: (info[CORE] ^ foreign, p, 0, 0)
    )
    shape = jax.ShapeDtypeStruct((outs, count), F32)
    return pl.pallas_call(
        functools.partial(update_kernel, foreign),
        grid_spec=pltpu.PrefetchScalarGridSpec(
            num_scalar_prefetch=1,
            grid=(pairs,),
            in_specs=[whole] * 4 + [kern_spec] * 4,
            out_specs=[whole, whole],
        ),
        out_shape=[shape, shape],
        compiler_params=params(),
        name="update",
    )(info, delta, index, weights, fitted, *own, *other)


def local(points, weights, targets, fitted, preconditioner, owners, block_index):
    steps, block = block_index.shape
    features = points.shape[1]
    outs = weights.shape[0]
    cores = GRID[2]
    groups = GRID[0] * GRID[1]
    lines = lax.axis_size("x")
    core = lax.axis_index("c")
    zy = lax.axis_index(ZY)
    rank = zy * cores + core

    given = lax.all_gather(preconditioner, DP, axis=0)
    owns = (owners == rank).astype(jnp.int32)
    same = (owners[0] == owners[1]).astype(jnp.int32)
    info = jnp.stack([core, lax.axis_index("x"), owns[0], owns[1], same])
    index = block_index.reshape(steps, block // LANES, LANES)

    keep, send = pick_blocks(info, points, index)
    got = exchange(send)
    owner_core = (owners % cores).reshape(steps, 1, 1)
    parcels = jnp.where(owner_core == core, keep, got)
    parcels = all_to_all(parcels.reshape(groups, -1, LANES), ZY)
    holder = owners[zy // (groups // steps)] // cores
    piece = lax.dynamic_index_in_dim(parcels, holder, 0)
    blocks = all_to_all(jnp.broadcast_to(piece, parcels.shape), ZY)
    blocks = blocks.reshape(1, steps * FEATURE_ROWS, LANES)
    own = all_to_all(jnp.broadcast_to(blocks, (lines, *blocks.shape[1:])), "x")
    other = exchange(own)

    grad_own, *kern_own = kernel_and_gradient(0, info, points, weights, targets, index, own)
    grad_other, *kern_other = kernel_and_gradient(
        1, info, points, weights, targets, index, other
    )
    grad = jnp.stack([grad_own, grad_other]).transpose(3, 0, 1, 2, 4)
    grad = all_to_all(grad.reshape(outs, -1, LANES), ZY)
    grad = jnp.sum(grad, axis=0)
    theirs = exchange(grad)
    between = between_blocks(features, info, index, own, other)
    delta = run_chain(info, grad, theirs, given, between)

    mine = lax.dynamic_index_in_dim(delta, core, 0)
    mine = all_to_all(jnp.broadcast_to(mine, (groups, *mine.shape[1:])), ZY)
    theirs = exchange(mine)
    weights, fitted = update(0, info, mine, index, weights, fitted, kern_own, kern_other)
    weights, fitted = update(1, info, theirs, index, weights, fitted, kern_own, kern_other)
    return (weights, fitted)


def solution(mesh):
    grid = Mesh(mesh.devices.reshape(*GRID, mesh.shape["out"]), (*DP, "x"))
    return jax.shard_map(
        local,
        mesh=grid,
        in_specs=(
            P(DP, None),
            P("x", DP),
            P("x", DP),
            P("x", DP),
            P(None, DP, None),
            P(),
            P(),
        ),
        out_specs=(P("x", DP), P("x", DP)),
        check_vma=False,
    )
```

time: 763 us -> 194 us (0.25)
  waiting for transfers between devices: 556 us -> 27.5 us
  blocking collectives: 104 us -> 52 us
  starting transfers between devices: 0.3 us -> 43.9 us
  Pallas kernels: 0 us -> 39.6 us
  matrix products: 39.4 us -> 0 us
  local copies, waits for them, and re-layouts: 29.1 us -> 9.69 us
  other arithmetic: 18.4 us -> 2.69 us
    psum x3 -> x0, waiting for transfers between devices: 556 us -> none  [the longest x2 362 us: local(): grad = lax.psum(partial_sum + own_term, 'dp')]
    all_gather x2 -> x0, blocking collectives: 104 us -> none  [local(): delta = lax.all_gather(my_rows, 'dp', axis=1, tiled=True)]
    all_to_all x0 -> x3, blocking collectives: none -> 52 us  [all_to_all(): return lax.all_to_all(value, axes, 0, 0, tiled=True)]
    pallas_call x0 -> x7, Pallas kernels: none -> 39.6 us  [the longest x2 15.7 us: kernel_and_gradient(): pl.pallas_call(functools.partial(kernel_kernel, foreign), grid_spec=pltpu...]
    dot_general x8 -> x0, matrix products: 39.4 us -> none  [the longest x2 14 us: local(): partial_sum = jnp.dot(weights, kern, precision=lax.Precision.HIGHEST)]
    ppermute x0 -> x4, starting transfers between devices: none -> 26.7 us  [exchange(): return lax.ppermute(value, 'c', [(0, 1), (1, 0)])]
    all_to_all x0 -> x2, waiting for transfers between devices: none -> 25.7 us  [all_to_all(): return lax.all_to_all(value, axes, 0, 0, tiled=True)]
    gather x6 -> x0, local copies, waits for them, and re-layouts: 22.6 us -> none  [the longest x2 9.04 us: local(): candidate = points[index]]
  transfers between devices with their start and end apart: 3 -> 7, of which waited for: 3 -> 3; matrix products, arithmetic and copies ran while one was open for 3% -> 5% of each run, Pallas kernels for 0% -> 14%
where the time goes in v1:
time: 194 us
  blocking collectives  52 us (27%)
  starting transfers between devices  43.9 us (23%)
  Pallas kernels  39.6 us (20%)
  waiting for transfers between devices  27.5 us (14%)
  between operations  18.2 us (9%)
  local copies, waits for them, and re-layouts  9.69 us (5%)
  other arithmetic  2.69 us (1%)
    all_to_all x3, blocking collectives, all_to_all(): return lax.all_to_all(value, axes, 0, 0, tiled=True)  52 us
    ppermute x4, starting transfers between devices, exchange(): return lax.ppermute(value, 'c', [(0, 1), (1, 0)])  26.7 us
    all_to_all x2, waiting for transfers between devices, all_to_all(): return lax.all_to_all(value, axes, 0, 0, tiled=True)  25.7 us
    all_to_all x2, starting transfers between devices, all_to_all(): return lax.all_to_all(value, axes, 0, 0, tiled=True)  17.1 us
    pallas_call x2, Pallas kernels, kernel_and_gradient(): pl.pallas_call(functools.partial(kernel_kernel, foreign), grid_spec=pltpu...  15.7 us
    pallas_call x2, Pallas kernels, update(): pl.pallas_call(functools.partial(update_kernel, foreign), grid_spec=pltpu...  10.4 us
    pallas_call x1, Pallas kernels, run_chain(): pl.pallas_call(chain_kernel, grid_spec=pltpu.PrefetchScalarGridSpec(num_s...  7.13 us
    pallas_call x1, Pallas kernels, between_blocks(): pl.pallas_call(functools.partial(between_kernel, features), grid_spec=plt...  4.96 us
  transfers between devices with their start and end apart: 7, of which 3 were waited for; matrix products, arithmetic and copies ran while one was open for 5% of the time, Pallas kernels for 14%

profile of v1, /device:TPU:1, one launch (start us, length us, event | category | flops | bytes accessed | tf_op | source)
XLA Modules:
  0.0 193.5 jit_solution(11840620431121174627)
XLA Ops:
  7.2 0.0 all-gather.3.cloned.1.call-start
  7.2 0.7 all-gather.3.cloned.1.call-update
  7.9 1.4 fusion.2
  10.7 0.7 copy.22
  11.4 1.7 copy.17.points_ref
  13.1 0.7 fusion
  13.7 0.1 pad_add_fusion.info
  13.8 1.4 pick_blocks.1
  15.3 0.0 copy-start.4
  15.3 0.0 copy-start.5
  15.3 8.9 %collective-permute-start = (bf16[2,512,128]{2,1,0:T(8,128)(2,1)S(1)}, bf16[2,512,128]{2,1,0:T(8,128)(2,1)S(1)}, u32[]{:S(2)}, u32[]{:S(2)}) collective-permute-start(bf16[2,512,128]{2,1,0:T(8,128)(2,1)S(1)} %get-tuple-element.13), channel_id=1, source_target_pairs={{0,4},{4,0},{1,5},{5,1},{2,6},{6,2},{3,7},{7,3},{8,12},{12,8},{9,1... | collective-permute-start | bytes 786440 | tf_op jit(solution)/shard_map/ppermute | solution.py:31
  24.2 1.1 collective-permute-done
  25.4 0.8 broadcast_select_fusion
  26.1 10.9 %all-to-all-start = ((bf16[64,16,128]{2,1,0:T(8,128)(2,1)}), bf16[64,16,128]{2,1,0:T(8,128)(2,1)S(1)}, u32[]{:S(2)}, u32[]{:S(2)}) async-start(bf16[64,16,128]{2,1,0:T(8,128)(2,1)} %bitcast.2), calls=%async_computation | async-start | bytes 524288 | tf_op jit(solution)/shard_map/all_to_all | solution.py:35
  39.7 10.3 %all-to-all-done = bf16[64,16,128]{2,1,0:T(8,128)(2,1)S(1)} async-done(((bf16[64,16,128]{2,1,0:T(8,128)(2,1)}), bf16[64,16,128]{2,1,0:T(8,128)(2,1)S(1)}, u32[]{:S(2)}, u32[]{:S(2)}) %all-to-all-start) | async-done | bytes 262176 | tf_op jit(solution)/shard_map/all_to_all | solution.py:35
  50.0 18.5 %all_to_all.25 = bf16[64,16,128]{2,1,0:T(8,128)(2,1)S(1)} all-to-all(bf16[64,16,128]{2,1,0:T(8,128)(2,1)S(1)} %broadcast_in_dim.31), channel_id=1, replica_groups=mesh['z'=8,'y'=8,'c'=2,'x'=4] {'z','y'}, dimensions={0} | all-to-all | bytes 524288 | tf_op jit(solution)/shard_map/all_to_all | solution.py:35
  68.5 0.1 broadcast_in_dim.33
  68.7 15.3 %all_to_all.26.blocks_ref.own_ref = bf16[4,1024,128]{2,1,0:T(8,128)(2,1)S(1)} all-to-all(bf16[4,1024,128]{2,1,0:T(8,128)(2,1)S(1)} %broadcast_in_dim.33), channel_id=1, replica_groups=mesh['z'=8,'y'=8,'c'=2,'x'=4] {'x'}, dimensions={0} | all-to-all | bytes 2097152 | tf_op jit(solution)/shard_map/all_to_all | solution.py:35
  83.9 6.6 %collective-permute-start.1 = (bf16[4,1024,128]{2,1,0:T(8,128)(2,1)S(1)}, bf16[4,1024,128]{2,1,0:T(8,128)(2,1)S(1)}, u32[]{:S(2)}, u32[]{:S(2)}) collective-permute-start(bf16[4,1024,128]{2,1,0:T(8,128)(2,1)S(1)} %all_to_all.26.blocks_ref.own_ref), channel_id=1, source_target_pairs={{0,4},{4,0},{1,5},{5,1},{2,6},{6,2},{3,7},{7,3},{8,12},{12,8},{9,1... | collective-permute-start | bytes 3145736 | tf_op jit(solution)/shard_map/ppermute | solution.py:31
  90.5 0.0 copy-done.4
  90.5 0.0 copy-done.5
  90.5 7.8 %kernel_and_gradient.2 = (f32[2,2,64,256]{3,2,1,0:T(8,128)S(1)}, bf16[2,2,1536,256]{3,2,1,0:T(8,128)(2,1)}, bf16[2,2,1536,256]{3,2,1,0:T(8,128)(2,1)}) custom-call(s32[5]{0:T(128)S(1)} %pad_add_fusion.info, bf16[1536,440]{1,0:T(8,128)(2,1)S(1)} %copy.17.points_ref, f32[64,1536]{1,0:T(8,128)S(1)} %copy-done.4, f32[64,1536]{1,0:T(8,128)S(1)} %copy-done.5, ...), custom_call_target="tpu_custom_call" | custom-call | tf_op jit(solution)/shard_map/kernel_and_gradient/pallas_call | solution.py:159
  98.4 0.0 collective-permute-done.1.blocks_ref.other_ref
  98.4 0.0 copy-start.2
  98.4 7.9 %kernel_and_gradient.3 = (f32[2,2,64,256]{3,2,1,0:T(8,128)S(1)}, bf16[2,2,1536,256]{3,2,1,0:T(8,128)(2,1)}, bf16[2,2,1536,256]{3,2,1,0:T(8,128)(2,1)}) custom-call(s32[5]{0:T(128)S(1)} %pad_add_fusion.info, bf16[1536,440]{1,0:T(8,128)(2,1)S(1)} %copy.17.points_ref, f32[64,1536]{1,0:T(8,128)S(1)} %copy-done.4, f32[64,1536]{1,0:T(8,128)S(1)} %copy-done.5, ...), custom_call_target="tpu_custom_call" | custom-call | tf_op jit(solution)/shard_map/kernel_and_gradient/pallas_call | solution.py:159
  106.3 0.0 copy-done.2
  106.3 0.0 copy-start.3
  106.3 1.2 copy.19
  107.6 2.3 %reshape.23 = f32[64,16,128]{2,1,0:T(8,128)} reshape(f32[64,2,2,2,256]{4,3,2,1,0:T(2,128)} %copy.19) | data formatting | bytes 1048576 | tf_op jit(solution)/shard_map/reshape | solution.py:419
  109.8 6.2 %all-to-all-start.3 = ((f32[64,16,128]{2,1,0:T(8,128)}), f32[64,16,128]{2,1,0:T(8,128)}, u32[]{:S(2)}, u32[]{:S(2)}) async-start(f32[64,16,128]{2,1,0:T(8,128)} %reshape.23), calls=%async_computation.3 | async-start | bytes 1048576 | tf_op jit(solution)/shard_map/all_to_all | solution.py:35
  116.0 15.4 %all-to-all-done.3 = f32[64,16,128]{2,1,0:T(8,128)} async-done(((f32[64,16,128]{2,1,0:T(8,128)}), f32[64,16,128]{2,1,0:T(8,128)}, u32[]{:S(2)}, u32[]{:S(2)}) %all-to-all-start.3) | async-done | bytes 524320 | tf_op jit(solution)/shard_map/all_to_all | solution.py:35
  131.4 1.1 reduce_sum.9.mine_ref
  132.5 7.2 %collective-permute-start.2 = (f32[16,128]{1,0:T(8,128)S(1)}, f32[16,128]{1,0:T(8,128)S(1)}, u32[]{:S(2)}, u32[]{:S(2)}) collective-permute-start(f32[16,128]{1,0:T(8,128)S(1)} %reduce_sum.9.mine_ref), channel_id=1, source_target_pairs={{0,4},{4,0},{1,5},{5,1},{2,6},{6,2},{3,7},{7,3},{8,12},{12,8},{9,1... | collective-permute-start | bytes 24584 | tf_op jit(solution)/shard_map/ppermute | solution.py:31
  139.8 0.0 copy-done.3
  139.8 5.0 %between_blocks.1.between_ref = f32[1024,1024]{1,0:T(8,128)} custom-call(s32[5]{0:T(128)S(1)} %pad_add_fusion.info, s32[2,8,128]{2,1,0:T(8,128)S(1)} %bitcast.21, bf16[4,1024,128]{2,1,0:T(8,128)(2,1)S(1)} %all_to_all.26.blocks_ref.own_ref, bf16[4,1024,128]{2,1,0:T(8,128)(2,1)S(1)} %copy-done.3), custom_call_target="tpu_custom_call" | custom-call | flops 1073741824 | bytes 4194304 | tf_op jit(solution)/shard_map/between_blocks/pallas_call | solution.py:222
  144.7 0.0 collective-permute-done.2.theirs_ref
  144.7 0.0 all-gather.3.cloned.1.call-done
  144.7 0.0 copy-start
  144.7 2.2 %copy-done = f32[1024,1024]{1,0:T(8,128)S(1)} copy-done((f32[1024,1024]{1,0:T(8,128)S(1)}, f32[1024,1024]{1,0:T(8,128)}, u32[]{:S(2)}) %copy-start) | copy-done | bytes 4194328
  146.9 0.0 copy-start.1
  146.9 0.0 copy-start.6
  146.9 7.1 %run_chain.1 = f32[2,8,128]{2,1,0:T(8,128)S(1)} custom-call(s32[5]{0:T(128)S(1)} %pad_add_fusion.info, f32[16,128]{1,0:T(8,128)S(1)} %reduce_sum.9.mine_ref, f32[16,128]{1,0:T(8,128)S(1)} %collective-permute-done.2.theirs_ref, f32[128,2,8,1024]{3,2,1,0:T(8,128)} %bitcast.26, f32[1024,1024]{1,0:T(8,128)S(1)} %copy-done), custom_call_target="tpu_custom_call" | custom-call | tf_op jit(solution)/shard_map/run_chain/pallas_call | solution.py:288
  154.1 18.2 %all_to_all.27.delta_ref = f32[64,8,128]{2,1,0:T(8,128)S(1)} all-to-all(f32[64,8,128]{2,1,0:T(8,128)S(1)} %broadcast_in_dim.35), channel_id=1, replica_groups=mesh['z'=8,'y'=8,'c'=2,'x'=4] {'z','y'}, dimensions={0} | all-to-all | bytes 524288 | tf_op jit(solution)/shard_map/all_to_all | solution.py:35
  172.3 4.0 %collective-permute-start.3 = (f32[64,8,128]{2,1,0:T(8,128)S(1)}, f32[64,8,128]{2,1,0:T(8,128)S(1)}, u32[]{:S(2)}, u32[]{:S(2)}) collective-permute-start(f32[64,8,128]{2,1,0:T(8,128)S(1)} %all_to_all.27.delta_ref), channel_id=1, source_target_pairs={{0,4},{4,0},{1,5},{5,1},{2,6},{6,2},{3,7},{7,3},{8,12},{12,8},{9,1... | collective-permute-start | bytes 786440 | tf_op jit(solution)/shard_map/ppermute | solution.py:31
  176.3 0.0 copy-done.1
  176.3 0.0 copy-done.6
  176.3 4.8 %update.2 = (f32[64,1536]{1,0:T(8,128)S(1)}, f32[64,1536]{1,0:T(8,128)S(1)}) custom-call(s32[5]{0:T(128)S(1)} %pad_add_fusion.info, f32[64,8,128]{2,1,0:T(8,128)S(1)} %all_to_all.27.delta_ref, s32[2,8,128]{2,1,0:T(8,128)S(1)} %bitcast.22, f32[64,1536]{1,0:T(8,128)S(1)} %copy-done.4, f32[64,1536]{1,0:T(8,128)S(1)} %copy-done.6, ...), custom_call_target="tpu_custom_call" | custom-call | tf_op jit(solution)/shard_map/update/pallas_call | solution.py:371
  181.1 0.0 collective-permute-done.3.delta_ref
  181.1 5.6 %update.3 = (f32[64,1536]{1,0:T(8,128)}, f32[64,1536]{1,0:T(8,128)}) custom-call(s32[5]{0:T(128)S(1)} %pad_add_fusion.info, f32[64,8,128]{2,1,0:T(8,128)S(1)} %collective-permute-done.3.delta_ref, s32[2,8,128]{2,1,0:T(8,128)S(1)} %bitcast.23, f32[64,1536]{1,0:T(8,128)S(1)} %get-tuple-element.20.weights_ref, f32[64,1536]{1,0:T(8,128)S(1)} %get-tuple-element.21.fitted_ref, ...), custom_call_target="tpu_custom_call" | custom-call | tf_op jit(solution)/shard_map/update/pallas_call | solution.py:371
  (5 shorter events, 0.1 us)
Async XLA Ops:
  7.2 137.6 %all-gather.3.cloned.1.call-start = ((), (), s32[]{:S(2)}) async-start(), calls=%async_computation.5 | async-start | bytes 8454144 | tf_op jit(solution)/shard_map/all_gather | solution.py:396
  15.3 75.3 %copy-start.4 = (f32[64,1536]{1,0:T(8,128)S(1)}, f32[64,1536]{1,0:T(8,128)}, u32[]{:S(2)}) copy-start(f32[64,1536]{1,0:T(8,128)} %weights_ref.5) | copy-start | bytes 1179652
  15.3 75.3 %copy-start.5 = (f32[64,1536]{1,0:T(8,128)S(1)}, f32[64,1536]{1,0:T(8,128)}, u32[]{:S(2)}) copy-start(f32[64,1536]{1,0:T(8,128)} %targets_ref.3) | copy-start | bytes 1179652
  15.3 10.1 %collective-permute-start = (bf16[2,512,128]{2,1,0:T(8,128)(2,1)S(1)}, bf16[2,512,128]{2,1,0:T(8,128)(2,1)S(1)}, u32[]{:S(2)}, u32[]{:S(2)}) collective-permute-start(bf16[2,512,128]{2,1,0:T(8,128)(2,1)S(1)} %get-tuple-element.13), channel_id=1, source_target_pairs={{0,4},{4,0},{1,5},{5,1},{2,6},{6,2},{3,7},{7,3},{8,12},{12,8},{9,1... | collective-permute-start | bytes 786440 | tf_op jit(solution)/shard_map/ppermute | solution.py:31
  26.1 23.8 %all-to-all-start = ((bf16[64,16,128]{2,1,0:T(8,128)(2,1)}), bf16[64,16,128]{2,1,0:T(8,128)(2,1)S(1)}, u32[]{:S(2)}, u32[]{:S(2)}) async-start(bf16[64,16,128]{2,1,0:T(8,128)(2,1)} %bitcast.2), calls=%async_computation | async-start | bytes 524288 | tf_op jit(solution)/shard_map/all_to_all | solution.py:35
  83.9 14.4 %collective-permute-start.1 = (bf16[4,1024,128]{2,1,0:T(8,128)(2,1)S(1)}, bf16[4,1024,128]{2,1,0:T(8,128)(2,1)S(1)}, u32[]{:S(2)}, u32[]{:S(2)}) collective-permute-start(bf16[4,1024,128]{2,1,0:T(8,128)(2,1)S(1)} %all_to_all.26.blocks_ref.own_ref), channel_id=1, source_target_pairs={{0,4},{4,0},{1,5},{5,1},{2,6},{6,2},{3,7},{7,3},{8,12},{12,8},{9,1... | collective-permute-start | bytes 3145736 | tf_op jit(solution)/shard_map/ppermute | solution.py:31
  98.4 7.9 %copy-start.2 = (bf16[4,1024,128]{2,1,0:T(8,128)(2,1)}, bf16[4,1024,128]{2,1,0:T(8,128)(2,1)S(1)}, u32[]{:S(2)}) copy-start(bf16[4,1024,128]{2,1,0:T(8,128)(2,1)S(1)} %collective-permute-done.1.blocks_ref.other_ref) | copy-start | bytes 3145732
  106.3 33.5 %copy-start.3 = (bf16[4,1024,128]{2,1,0:T(8,128)(2,1)S(1)}, bf16[4,1024,128]{2,1,0:T(8,128)(2,1)}, u32[]{:S(2)}) copy-start(bf16[4,1024,128]{2,1,0:T(8,128)(2,1)} %copy-done.2) | copy-start | bytes 3145732
  109.8 21.6 %all-to-all-start.3 = ((f32[64,16,128]{2,1,0:T(8,128)}), f32[64,16,128]{2,1,0:T(8,128)}, u32[]{:S(2)}, u32[]{:S(2)}) async-start(f32[64,16,128]{2,1,0:T(8,128)} %reshape.23), calls=%async_computation.3 | async-start | bytes 1048576 | tf_op jit(solution)/shard_map/all_to_all | solution.py:35
  132.5 12.2 %collective-permute-start.2 = (f32[16,128]{1,0:T(8,128)S(1)}, f32[16,128]{1,0:T(8,128)S(1)}, u32[]{:S(2)}, u32[]{:S(2)}) collective-permute-start(f32[16,128]{1,0:T(8,128)S(1)} %reduce_sum.9.mine_ref), channel_id=1, source_target_pairs={{0,4},{4,0},{1,5},{5,1},{2,6},{6,2},{3,7},{7,3},{8,12},{12,8},{9,1... | collective-permute-start | bytes 24584 | tf_op jit(solution)/shard_map/ppermute | solution.py:31
  144.7 2.2 %copy-start = (f32[1024,1024]{1,0:T(8,128)S(1)}, f32[1024,1024]{1,0:T(8,128)}, u32[]{:S(2)}) copy-start(f32[1024,1024]{1,0:T(8,128)} %between_blocks.1.between_ref) | copy-start | bytes 12582916
  146.9 29.4 %copy-start.1 = (bf16[2,2,1536,256]{3,2,1,0:T(8,128)(2,1)S(1)}, bf16[2,2,1536,256]{3,2,1,0:T(8,128)(2,1)}, u32[]{:S(2)}) copy-start(bf16[2,2,1536,256]{3,2,1,0:T(8,128)(2,1)} %get-tuple-element.16.own_high) | copy-start | bytes 9437188
  146.9 29.4 %copy-start.6 = (f32[64,1536]{1,0:T(8,128)S(1)}, f32[64,1536]{1,0:T(8,128)}, u32[]{:S(2)}) copy-start(f32[64,1536]{1,0:T(8,128)} %fitted_ref.1) | copy-start | bytes 1179652
  172.3 8.8 %collective-permute-start.3 = (f32[64,8,128]{2,1,0:T(8,128)S(1)}, f32[64,8,128]{2,1,0:T(8,128)S(1)}, u32[]{:S(2)}, u32[]{:S(2)}) collective-permute-start(f32[64,8,128]{2,1,0:T(8,128)S(1)} %all_to_all.27.delta_ref), channel_id=1, source_target_pairs={{0,4},{4,0},{1,5},{5,1},{2,6},{6,2},{3,7},{7,3},{8,12},{12,8},{9,1... | collective-permute-start | bytes 786440 | tf_op jit(solution)/shard_map/ppermute | solution.py:31
Sparse Core Ops, SparseCore 0:
  11.1 97.4 all-gather.2

commit v2 on v0

v2 whole, which is shorter than its diff:
```python
import functools

import jax
import jax.numpy as jnp
from jax import lax
from jax.experimental import pallas as pl
from jax.experimental.pallas import tpu as pltpu
from jax.sharding import Mesh, PartitionSpec as P

LAMBDA = 0.5
GRID = (8, 8, 2)
ZY = ("z", "y")
DP = ("z", "y", "c")
FEATURE_ROWS = 512
LANES = 128
CHUNK = 256
UNIT = 768
VMEM_BYTES = 16 * 1024 * 1024
BF16 = jnp.bfloat16
F32 = jnp.float32
TRANSPOSED = (((1,), (1,)), ((), ()))
FIRST_DIMS = (((0,), (0,)), ((), ()))
WHOLE = pl.BlockSpec(memory_space=pltpu.VMEM)


def call(kernel, name, shapes, owners, *args, scratch=(), aliases=None, cost=None):
    return pl.pallas_call(
        kernel,
        grid_spec=pltpu.PrefetchScalarGridSpec(
            num_scalar_prefetch=1,
            grid=(),
            in_specs=[WHOLE] * len(args),
            out_specs=[WHOLE] * len(shapes),
            scratch_shapes=list(scratch),
        ),
        out_shape=[jax.ShapeDtypeStruct(*shape) for shape in shapes],
        input_output_aliases=aliases or {},
        compiler_params=pltpu.CompilerParams(vmem_limit_bytes=VMEM_BYTES),
        cost_estimate=cost,
        name=name,
    )(owners, *args)


def my_rank():
    return (lax.axis_index("z") * GRID[1] + lax.axis_index("y")) * GRID[2] + lax.axis_index("c")


def exchange(value):
    return lax.ppermute(value, "c", [(0, 1), (1, 0)])


def all_to_all(value, axes):
    return lax.all_to_all(value, axes, 0, 0, tiled=True)


def two_parts(value):
    high = value.astype(BF16)
    return high, (value - high.astype(F32)).astype(BF16)


def three_parts(value):
    high = value.astype(BF16)
    rest = value - high.astype(F32)
    middle = rest.astype(BF16)
    return high, middle, (rest - middle.astype(F32)).astype(BF16)


def dot(left, right, dims=(((1,), (0,)), ((), ()))):
    return lax.dot_general(left, right, dims, preferred_element_type=F32)


def one_hot(count, numbers):
    rows = lax.broadcasted_iota(jnp.int32, (count, numbers.shape[1]), 0)
    return jnp.where(rows == numbers, 1.0, 0.0).astype(BF16)


def index_tile(index_ref, step, line, kind):
    at = pl.multiple_of((2 * line + kind) * LANES, LANES)
    tiles = index_ref[:, pl.ds(at, LANES)]
    return jnp.where(step == 0, tiles[0:1], tiles[1:2])


def pick_kernel(owners, points_ref, index_ref, keep_ref, send_ref):
    features, count = points_ref.shape
    steps = index_ref.shape[0]
    core, line = lax.axis_index("c"), lax.axis_index("x")
    numbers = [
        index_tile(index_ref, step, line, kind)
        for kind in (core, 1 - core)
        for step in range(steps)
    ]
    picked = dot(points_ref[...], one_hot(count, jnp.concatenate(numbers, axis=1)))
    empty = jnp.zeros((FEATURE_ROWS - features, picked.shape[1]), F32)
    picked = jnp.concatenate([picked, empty], axis=0).astype(BF16)
    for place, ref in enumerate((keep_ref, send_ref)):
        for step in range(steps):
            at = (place * steps + step) * LANES
            ref[step] = picked[:, at : at + LANES]


def pick_blocks(owners, points, index):
    shape = ((index.shape[0], FEATURE_ROWS, LANES), BF16)
    return call(pick_kernel, "pick_blocks", [shape, shape], owners, points.T, index)


def kernel_kernel(
    foreign,
    owners,
    points_ref,
    weights_ref,
    targets_ref,
    index_ref,
    blocks_ref,
    grad_ref,
    high_ref,
    low_ref,
    parts,
    norms,
):
    count, features = points_ref.shape
    outs = weights_ref.shape[0]
    pairs = blocks_ref.shape[0] // 2
    steps = index_ref.shape[0]
    gamma = 2.0 / features
    high, low = two_parts(weights_ref[...])
    parts[:outs, :] = high
    parts[outs:, :] = low
    for at in range(0, count, CHUNK):
        wide = points_ref[at : at + CHUNK, :].astype(F32)
        norms[at : at + CHUNK, :] = gamma * jnp.sum(wide * wide, axis=1, keepdims=True)

    blocks, block_norms, grads = [], [], []
    for step in range(steps):
        rows = slice(step * FEATURE_ROWS, (step + 1) * FEATURE_ROWS)
        for pair in range(pairs):
            block = jnp.concatenate(
                [blocks_ref[2 * pair, rows, :], blocks_ref[2 * pair + 1, rows, :]], axis=1
            )
            wide = block.astype(F32)
            blocks.append(block[:features, :])
            block_norms.append(gamma * jnp.sum(wide * wide, axis=0, keepdims=True))
            grads.append(jnp.zeros((outs, 2 * LANES), F32))

    units = [(n, at) for n in range(steps * pairs) for at in range(0, count, UNIT)]

    def cross(n, at):
        return dot(points_ref[at : at + UNIT, :], blocks[n])

    ahead = cross(*units[0])
    for place, (n, at) in enumerate(units):
        now = ahead
        if place + 1 < len(units):
            ahead = cross(*units[place + 1])
        rows = slice(at, at + UNIT)
        kern = jnp.exp((2.0 * gamma) * now - (norms[rows, :] + block_norms[n]))
        high, low = two_parts(kern)
        high_ref[n, rows, :] = high
        low_ref[n, rows, :] = low
        both = dot(parts[:, rows], high)
        grads[n] += both[:outs] + both[outs:] + dot(parts[:outs, rows], low)

    def tiles(n):
        step, pair = divmod(n, pairs)
        return [(step * pairs + pair) * 2 + k for k in range(2)]

    for n, grad in enumerate(grads):
        for k, tile in enumerate(tiles(n)):
            part = grad[:, k * LANES : (k + 1) * LANES]
            grad_ref[:, tile : tile + 1, :] = part.reshape(outs, 1, LANES)

    rank = my_rank()
    kind = lax.axis_index("c") ^ foreign
    for step in range(steps):

        @pl.when(owners[step] == rank)
        def _():
            own = three_parts(LAMBDA * weights_ref[...] - targets_ref[...])
            for line in range(2 * pairs):
                pick = one_hot(count, index_tile(index_ref, step, line, kind))
                terms = [dot(part, pick) for part in own]
                tile = step * 2 * pairs + line
                grad_ref[:, tile : tile + 1, :] += (
                    terms[0] + (terms[1] + terms[2])
                ).reshape(outs, 1, LANES)


def kernel_and_gradient(foreign, owners, points, weights, targets, index, blocks):
    count = points.shape[0]
    outs = weights.shape[0]
    tiles = index.shape[0] * blocks.shape[0]
    kern = ((tiles // 2, count, 2 * LANES), BF16)
    return call(
        functools.partial(kernel_kernel, foreign),
        "kernel_and_gradient",
        [((outs, tiles, LANES), F32), kern, kern],
        owners,
        points,
        weights,
        targets,
        index,
        blocks,
        scratch=[pltpu.VMEM((2 * outs, count), BF16), pltpu.VMEM((count, 1), F32)],
        cost=pl.CostEstimate(
            flops=tiles * LANES * count * (2 * FEATURE_ROWS + 6 * outs),
            bytes_accessed=4 * tiles * LANES * count,
            transcendentals=tiles * LANES * count,
        ),
    )


def between_kernel(features, owners, index_ref, own_ref, other_ref, out_ref):
    lines = own_ref.shape[0]
    gamma = 2.0 / features
    core = lax.axis_index("c")

    def tile(step, line, kind):
        at = step * FEATURE_ROWS
        rows = slice(at, at + FEATURE_ROWS)
        return jnp.where(core == kind, own_ref[line, rows, :], other_ref[line, rows, :])

    places = [(line, kind) for line in range(lines) for kind in range(2)]
    second = jnp.concatenate([tile(1, *place) for place in places], axis=1)
    wide = second.astype(F32)
    second_norm = gamma * jnp.sum(wide * wide, axis=0, keepdims=True)
    second_index = index_ref[1:2, :]
    extra = jnp.where(owners[0] == owners[1], LAMBDA, 0.0)
    for n, place in enumerate(places):
        first = tile(0, *place)
        wide = first.astype(F32)
        square = jnp.sum(wide * wide, axis=0, keepdims=True)
        first_norm = gamma * jnp.transpose(jnp.broadcast_to(square, (LANES, LANES)))[:, :1]
        first_index = jnp.transpose(
            jnp.broadcast_to(
                index_ref[0:1, n * LANES : (n + 1) * LANES].astype(F32), (LANES, LANES)
            )
        )[:, :1].astype(jnp.int32)
        cross = dot(first, second, FIRST_DIMS)
        kern = jnp.exp((2.0 * gamma) * cross - (first_norm + second_norm))
        out_ref[n * LANES : (n + 1) * LANES, :] = kern + jnp.where(
            first_index == second_index, extra, 0.0
        )


def between_blocks(features, owners, index, own, other):
    block = index.shape[1]
    return call(
        functools.partial(between_kernel, features),
        "between_blocks",
        [((block, block), F32)],
        owners,
        index,
        own,
        other,
        cost=pl.CostEstimate(
            flops=2 * block * block * FEATURE_ROWS,
            bytes_accessed=4 * block * block,
            transcendentals=block * block,
        ),
    )[0]


def chain_kernel(owners, mine_ref, theirs_ref, given_ref, between_ref, out_ref, grads):
    tiles = out_ref.shape[1]
    block = between_ref.shape[0]
    rows = given_ref.shape[2]
    lines = tiles // 2
    core = lax.axis_index("c")
    for step in range(2):
        for line in range(lines):
            at = slice(step * lines + line, step * lines + line + 1)
            for kind in range(2):
                lanes = slice((2 * line + kind) * LANES, (2 * line + kind + 1) * LANES)
                grads[step : step + 1, lanes] = jnp.where(
                    core == kind, theirs_ref[at, :], mine_ref[at, :]
                )

    diagonal = lax.broadcasted_iota(jnp.int32, (LANES, LANES), 0) == lax.broadcasted_iota(
        jnp.int32, (LANES, LANES), 1
    )
    share = LANES // rows
    correction = jnp.zeros((8, block), F32)
    for step in range(2):
        grad = grads[step : step + 1, :]
        if step == 1:
            grad = grad - jnp.sum(correction, axis=0, keepdims=True)
        for n in range(tiles):
            given = given_ref[n * share : (n + 1) * share, step].reshape(LANES, block)
            delta = jnp.sum(given * grad, axis=1, keepdims=True)
            row = jnp.sum(jnp.where(diagonal, delta, 0.0), axis=0, keepdims=True)
            out_ref[step, n : n + 1, :] = row
            if step == 0:
                product = delta * between_ref[n * LANES : (n + 1) * LANES, :]
                correction += jnp.sum(product.reshape(-1, 8, block), axis=0)


def run_chain(owners, mine, theirs, given, between):
    block = given.shape[3]
    return call(
        chain_kernel,
        "run_chain",
        [((2, block // LANES, LANES), F32)],
        owners,
        mine,
        theirs,
        given,
        between,
        scratch=[pltpu.VMEM((2, block), F32)],
    )[0]


def update_kernel(
    foreign,
    owners,
    delta_ref,
    index_ref,
    weights_ref,
    fitted_ref,
    own_high,
    own_low,
    other_high,
    other_low,
    new_weights_ref,
    new_fitted_ref,
):
    core = lax.axis_index("c")
    step = core ^ foreign
    outs, count = weights_ref.shape
    pairs = own_high.shape[0] // 2

    deltas = []
    for pair in range(pairs):
        for kind in (core, 1 - core):
            tiles = [
                delta_ref[:, pl.ds(2 * (2 * pair + k) + kind, 1), :].reshape(outs, LANES)
                for k in range(2)
            ]
            deltas.append((pair, kind, jnp.concatenate(tiles, axis=1)))
    parts = [two_parts(delta) for _, _, delta in deltas]
    both = [jnp.concatenate(part, axis=0) for part in parts]
    for at in range(0, count, CHUNK):
        rows = slice(at, at + CHUNK)
        total = jnp.zeros((2 * outs, CHUNK), F32)
        small = jnp.zeros((outs, CHUNK), F32)
        for n, (pair, _, _) in enumerate(deltas):
            high_ref, low_ref = ((own_high, own_low), (other_high, other_low))[n % 2]
            total += dot(both[n], high_ref[step * pairs + pair, rows, :], TRANSPOSED)
            small += dot(parts[n][0], low_ref[step * pairs + pair, rows, :], TRANSPOSED)
        new_fitted_ref[:, rows] = fitted_ref[:, rows] - (
            total[:outs] + (total[outs:] + small)
        )

    new_weights_ref[...] = weights_ref[...]

    @pl.when(owners[step] == my_rank())
    def _():
        for pair, kind, delta in deltas:
            numbers = [index_tile(index_ref, step, 2 * pair + k, kind) for k in range(2)]
            pick = one_hot(count, jnp.concatenate(numbers, axis=1))
            terms = [dot(part, pick, TRANSPOSED) for part in three_parts(delta)]
            new_weights_ref[...] -= terms[0] + (terms[1] + terms[2])


def update(foreign, owners, delta, index, weights, fitted, own, other):
    shape = (weights.shape, F32)
    return call(
        functools.partial(update_kernel, foreign),
        "update",
        [shape, shape],
        owners,
        delta,
        index,
        weights,
        fitted,
        *own,
        *other,
        cost=pl.CostEstimate(
            flops=6 * own[0].size * weights.shape[0],
            bytes_accessed=4 * own[0].size,
            transcendentals=0,
        ),
    )


def local(points, weights, targets, fitted, preconditioner, owners, block_index):
    steps = block_index.shape[0]
    features = points.shape[1]
    groups = GRID[0] * GRID[1]
    lines = lax.axis_size("x")
    core = lax.axis_index("c")
    per_step = (groups // steps).bit_length() - 1

    given = lax.all_gather(preconditioner, DP, axis=0)

    keep, send = pick_blocks(owners, points, block_index)
    got = exchange(send)
    owner_core = (owners & 1).reshape(steps, 1, 1)
    parcels = jnp.where(owner_core == core, keep, got)
    parcels = all_to_all(parcels.reshape(groups, -1, LANES), ZY)
    late = lax.axis_index(ZY) >> per_step
    holder = (jnp.where(late == 0, owners[0], owners[1]) >> 1).astype(jnp.uint32)
    zero = jnp.uint32(0)
    piece = lax.dynamic_slice(parcels, (holder, zero, zero), (1, *parcels.shape[1:]))
    blocks = all_to_all(jnp.broadcast_to(piece, parcels.shape), ZY)
    blocks = blocks.reshape(1, steps * FEATURE_ROWS, LANES)
    own = all_to_all(jnp.broadcast_to(blocks, (lines, *blocks.shape[1:])), "x")
    other = exchange(own)

    data = (points, weights, targets, block_index)
    grad_own, *kern_own = kernel_and_gradient(0, owners, *data, own)
    grad_theirs = exchange(grad_own)
    grad_other, *kern_other = kernel_and_gradient(1, owners, *data, other)
    grad = all_to_all(grad_other + grad_theirs, ZY)
    grad = jnp.sum(grad, axis=0)
    between = between_blocks(features, owners, block_index, own, other)
    grad, between = lax.optimization_barrier((grad, between))
    delta = run_chain(owners, grad, exchange(grad), given, between)

    mine = jnp.where(core == 0, delta[0], delta[1])[None]
    mine = all_to_all(jnp.broadcast_to(mine, (groups, *mine.shape[1:])), ZY)
    theirs = exchange(mine)
    rest = (kern_own, kern_other)
    weights, fitted = update(0, owners, mine, block_index, weights, fitted, *rest)
    weights, fitted = update(1, owners, theirs, block_index, weights, fitted, *rest)
    return (weights, fitted)


def solution(mesh):
    grid = Mesh(mesh.devices.reshape(*GRID, mesh.shape["out"]), (*DP, "x"))
    return jax.shard_map(
        local,
        mesh=grid,
        in_specs=(
            P(DP, None),
            P("x", DP),
            P("x", DP),
            P("x", DP),
            P(None, DP, None),
            P(),
            P(),
        ),
        out_specs=(P("x", DP), P("x", DP)),
        check_vma=False,
    )
```

time: 763 us -> 182 us (0.24)
  waiting for transfers between devices: 556 us -> 20.8 us
  blocking collectives: 104 us -> 50.8 us
  starting transfers between devices: 0.3 us -> 43.9 us
  matrix products: 39.4 us -> 0 us
  Pallas kernels: 0 us -> 26.2 us
  other arithmetic: 18.4 us -> 3.21 us
  local copies, waits for them, and re-layouts: 29.1 us -> 20.8 us
    psum x3 -> x0, waiting for transfers between devices: 556 us -> none  [the longest x2 362 us: local(): grad = lax.psum(partial_sum + own_term, 'dp')]
    all_gather x2 -> x0, blocking collectives: 104 us -> none  [local(): delta = lax.all_gather(my_rows, 'dp', axis=1, tiled=True)]
    all_to_all x0 -> x3, blocking collectives: none -> 50.8 us  [all_to_all(): return lax.all_to_all(value, axes, 0, 0, tiled=True)]
    dot_general x8 -> x0, matrix products: 39.4 us -> none  [the longest x2 14 us: local(): partial_sum = jnp.dot(weights, kern, precision=lax.Precision.HIGHEST)]
    pallas_call x0 -> x7, Pallas kernels: none -> 26.2 us  [call(): pl.pallas_call(kernel, grid_spec=pltpu.PrefetchScalarGridSpec(num_scalar_...]
    ppermute x0 -> x5, starting transfers between devices: none -> 25.4 us  [exchange(): return lax.ppermute(value, 'c', [(0, 1), (1, 0)])]
    gather x6 -> x0, local copies, waits for them, and re-layouts: 22.6 us -> none  [the longest x2 9.04 us: local(): candidate = points[index]]
    all_to_all x0 -> x2, waiting for transfers between devices: none -> 18.7 us  [all_to_all(): return lax.all_to_all(value, axes, 0, 0, tiled=True)]
  transfers between devices with their start and end apart: 3 -> 8, of which waited for: 3 -> 4; matrix products, arithmetic and copies ran while one was open for 3% -> 3% of each run, Pallas kernels for 0% -> 11%
where the time goes in v2:
time: 182 us; the launch traced here: 181 us
  blocking collectives  50.8 us (28%)
  starting transfers between devices  43.9 us (24%)
  Pallas kernels  26.2 us (14%)
  waiting for transfers between devices  20.8 us (11%)
  local copies, waits for them, and re-layouts  20.8 us (11%)
  between operations  15.5 us (9%)
  other arithmetic  3.21 us (2%)
    all_to_all x3, blocking collectives, all_to_all(): return lax.all_to_all(value, axes, 0, 0, tiled=True)  50.8 us
    pallas_call x7, Pallas kernels, call(): pl.pallas_call(kernel, grid_spec=pltpu.PrefetchScalarGridSpec(num_scalar_...  26.2 us
    ppermute x5, starting transfers between devices, exchange(): return lax.ppermute(value, 'c', [(0, 1), (1, 0)])  25.4 us
    unnamed x39, local copies, waits for them, and re-layouts  19.3 us
    all_to_all x2, waiting for transfers between devices, all_to_all(): return lax.all_to_all(value, axes, 0, 0, tiled=True)  18.7 us
    all_to_all x2, starting transfers between devices, all_to_all(): return lax.all_to_all(value, axes, 0, 0, tiled=True)  18.4 us
  transfers between devices with their start and end apart: 8, of which 4 were waited for; matrix products, arithmetic and copies ran while one was open for 3% of the time, Pallas kernels for 11%

profile of v2, /device:TPU:1, one launch (start us, length us, event | category | flops | bytes accessed | tf_op | source)
XLA Modules:
  0.0 181.2 jit_solution(16360610157732809553)
XLA Ops:
  7.2 0.0 all-gather.3.cloned.1.call-start
  7.2 0.7 all-gather.3.cloned.1.call-update
  7.9 0.0 copy-start.9
  7.9 1.3 copy-done.9
  9.2 0.0 copy-start.14
  9.2 0.7 copy-done.14
  9.9 0.0 copy-start.16
  9.9 0.7 copy-done.16
  10.6 0.0 copy-start.10
  10.6 1.4 pick_blocks.1
  12.0 8.8 %collective-permute-start = (bf16[2,512,128]{2,1,0:T(8,128)(2,1)S(1)}, bf16[2,512,128]{2,1,0:T(8,128)(2,1)S(1)}, u32[]{:S(2)}, u32[]{:S(2)}) collective-permute-start(bf16[2,512,128]{2,1,0:T(8,128)(2,1)S(1)} %get-tuple-element.15), channel_id=1, source_target_pairs={{0,4},{4,0},{1,5},{5,1},{2,6},{6,2},{3,7},{7,3},{8,12},{12,8},{9,1... | collective-permute-start | bytes 786440 | tf_op jit(solution)/shard_map/ppermute | solution.py:49
  20.8 0.7 and_compare_fusion
  21.5 0.5 collective-permute-done
  22.0 0.8 broadcast_select_fusion
  22.7 10.9 %all-to-all-start = ((bf16[64,16,128]{2,1,0:T(8,128)(2,1)}), bf16[64,16,128]{2,1,0:T(8,128)(2,1)S(1)}, u32[]{:S(2)}, u32[]{:S(2)}) async-start(bf16[64,16,128]{2,1,0:T(8,128)(2,1)} %bitcast.1), calls=%async_computation | async-start | bytes 524288 | tf_op jit(solution)/shard_map/all_to_all | solution.py:53
  33.7 1.3 fusion.1
  36.2 11.3 %all-to-all-done = bf16[64,16,128]{2,1,0:T(8,128)(2,1)S(1)} async-done(((bf16[64,16,128]{2,1,0:T(8,128)(2,1)}), bf16[64,16,128]{2,1,0:T(8,128)(2,1)S(1)}, u32[]{:S(2)}, u32[]{:S(2)}) %all-to-all-start) | async-done | bytes 262176 | tf_op jit(solution)/shard_map/all_to_all | solution.py:53
  47.6 17.8 %all_to_all.25 = bf16[64,16,128]{2,1,0:T(8,128)(2,1)S(1)} all-to-all(bf16[64,16,128]{2,1,0:T(8,128)(2,1)S(1)} %broadcast_in_dim.32), channel_id=1, replica_groups=mesh['z'=8,'y'=8,'c'=2,'x'=4] {'z','y'}, dimensions={0} | all-to-all | bytes 524288 | tf_op jit(solution)/shard_map/all_to_all | solution.py:53
  65.4 0.0 copy-start.12
  65.4 0.0 copy-start.15
  65.4 0.0 copy-start.17
  65.4 0.1 broadcast_in_dim.34
  65.5 15.5 %all_to_all.26.blocks_ref.own_ref = bf16[4,1024,128]{2,1,0:T(8,128)(2,1)} all-to-all(bf16[4,1024,128]{2,1,0:T(8,128)(2,1)S(1)} %broadcast_in_dim.34), channel_id=1, replica_groups=mesh['z'=8,'y'=8,'c'=2,'x'=4] {'x'}, dimensions={0} | all-to-all | bytes 2097152 | tf_op jit(solution)/shard_map/all_to_all | solution.py:53
  81.0 6.6 %collective-permute-start.1 = (bf16[4,1024,128]{2,1,0:T(8,128)(2,1)}, bf16[4,1024,128]{2,1,0:T(8,128)(2,1)}, u32[]{:S(2)}, u32[]{:S(2)}) collective-permute-start(bf16[4,1024,128]{2,1,0:T(8,128)(2,1)} %all_to_all.26.blocks_ref.own_ref), channel_id=1, source_target_pairs={{0,4},{4,0},{1,5},{5,1},{2,6},{6,2},{3,7},{7,3},{8,12},{12,8},{9,1... | collective-permute-start | bytes 3145736 | tf_op jit(solution)/shard_map/ppermute | solution.py:49
  87.7 0.0 copy-done.10
  87.7 1.6 copy.11.points_ref
  89.2 0.0 copy-done.12
  89.2 0.0 copy-done.15
  89.3 0.0 copy-done.17
  89.3 0.0 copy-start.11
  89.3 1.4 copy-done.11
  90.7 0.0 copy-start.18
  90.7 1.0 copy-done.18
  91.7 5.9 %kernel_and_gradient.3 = (f32[64,8,128]{2,1,0:T(8,128)S(1)}, bf16[4,1536,256]{2,1,0:T(8,128)(2,1)S(1)}, bf16[4,1536,256]{2,1,0:T(8,128)(2,1)S(1)}) custom-call(s32[2]{0:T(128)S(1)} %copy-done.17, bf16[1536,440]{1,0:T(8,128)(2,1)S(1)} %copy-done.11, f32[64,1536]{1,0:T(8,128)S(1)} %copy-done.12, f32[64,1536]{1,0:T(8,128)S(1)} %copy-done.18, ...), custom_call_target="tpu_custom_call" | custom-call | flops 2214592512 | bytes 6291456 | tf_op jit(solution)/shard_map/kernel_and_gradient/pallas_call | solution.py:27
  97.6 0.0 copy-start.2
  97.6 1.6 copy-done.2
  99.2 2.1 %collective-permute-start.2 = (f32[64,8,128]{2,1,0:T(8,128)S(1)}, f32[64,8,128]{2,1,0:T(8,128)S(1)}, u32[]{:S(2)}, u32[]{:S(2)}) collective-permute-start(f32[64,8,128]{2,1,0:T(8,128)S(1)} %get-tuple-element.17), channel_id=1, source_target_pairs={{0,4},{4,0},{1,5},{5,1},{2,6},{6,2},{3,7},{7,3},{8,12},{12,8},{9,1... | collective-permute-start | bytes 786440 | tf_op jit(solution)/shard_map/ppermute | solution.py:49
  101.3 0.0 collective-permute-done.1.blocks_ref.other_ref
  101.3 5.8 %kernel_and_gradient.2 = (f32[64,8,128]{2,1,0:T(8,128)S(1)}, bf16[4,1536,256]{2,1,0:T(8,128)(2,1)S(1)}, bf16[4,1536,256]{2,1,0:T(8,128)(2,1)S(1)}) custom-call(s32[2]{0:T(128)S(1)} %copy-done.17, bf16[1536,440]{1,0:T(8,128)(2,1)S(1)} %copy-done.11, f32[64,1536]{1,0:T(8,128)S(1)} %copy-done.12, f32[64,1536]{1,0:T(8,128)S(1)} %copy-done.18, ...), custom_call_target="tpu_custom_call" | custom-call | flops 2214592512 | bytes 6291456 | tf_op jit(solution)/shard_map/kernel_and_gradient/pallas_call | solution.py:27
  107.2 0.0 copy-start.4
  107.2 1.7 copy-done.4
  108.8 1.7 copy-done.6
  110.5 0.0 collective-permute-done.2
  110.5 0.7 add.7
  111.3 7.5 %all-to-all-start.3 = ((f32[64,8,128]{2,1,0:T(8,128)}), f32[64,8,128]{2,1,0:T(8,128)}, u32[]{:S(2)}, u32[]{:S(2)}) async-start(f32[64,8,128]{2,1,0:T(8,128)} %add.7), calls=%async_computation.3 | async-start | bytes 524288 | tf_op jit(solution)/shard_map/all_to_all | solution.py:53
  118.8 4.5 %between_blocks.1.between_ref = f32[1024,1024]{1,0:T(8,128)S(1)} custom-call(s32[2]{0:T(128)S(1)} %copy-done.17, s32[2,1024]{1,0:T(2,128)S(1)} %copy-done.15, bf16[4,1024,128]{2,1,0:T(8,128)(2,1)} %all_to_all.26.blocks_ref.own_ref, bf16[4,1024,128]{2,1,0:T(8,128)(2,1)} %collective-permute-done.1.blocks_ref.other_ref), custom_call_target="tpu_custom_call" | custom-call | flops 1073741824 | bytes 4194304 | tf_op jit(solution)/shard_map/between_blocks/pallas_call | solution.py:27
  123.3 0.0 copy-start
  123.3 2.0 %copy-done = f32[1024,1024]{1,0:T(8,128)} copy-done((f32[1024,1024]{1,0:T(8,128)}, f32[1024,1024]{1,0:T(8,128)S(1)}, u32[]{:S(2)}) %copy-start) | copy-done | bytes 4194328
  125.3 7.4 %all-to-all-done.3 = f32[64,8,128]{2,1,0:T(8,128)} async-done(((f32[64,8,128]{2,1,0:T(8,128)}), f32[64,8,128]{2,1,0:T(8,128)}, u32[]{:S(2)}, u32[]{:S(2)}) %all-to-all-start.3) | async-done | bytes 262176 | tf_op jit(solution)/shard_map/all_to_all | solution.py:53
  132.7 1.0 reduce_sum.9.mine_ref
  133.7 3.1 %collective-permute-start.3 = (f32[8,128]{1,0:T(8,128)S(1)}, f32[8,128]{1,0:T(8,128)}, u32[]{:S(2)}, u32[]{:S(2)}) collective-permute-start(f32[8,128]{1,0:T(8,128)S(1)} %reduce_sum.9.mine_ref), channel_id=1, source_target_pairs={{0,4},{4,0},{1,5},{5,1},{2,6},{6,2},{3,7},{7,3},{8,12},{12,8},{9,1... | collective-permute-start | bytes 12296 | tf_op jit(solution)/shard_map/ppermute | solution.py:49
  136.8 0.9 collective-permute-done.3.theirs_ref
  137.8 2.2 %copy-done.1 = f32[1024,1024]{1,0:T(8,128)S(1)} copy-done((f32[1024,1024]{1,0:T(8,128)S(1)}, f32[1024,1024]{1,0:T(8,128)}, u32[]{:S(2)}) %copy-start.1) | copy-done | bytes 4194328
  140.0 3.4 %copy-done.8 = f32[256,8,1024]{2,1,0:T(8,128)S(1)} copy-done((f32[256,8,1024]{2,1,0:T(8,128)S(1)}, f32[256,8,1024]{2,1,0:T(8,128)}, u32[]{:S(2)}) %copy-start.8) | copy-done | bytes 8388632
  143.3 2.5 %run_chain.1 = f32[2,8,128]{2,1,0:T(8,128)S(1)} custom-call(s32[2]{0:T(128)S(1)} %copy-done.17, f32[8,128]{1,0:T(8,128)S(1)} %reduce_sum.9.mine_ref, f32[8,128]{1,0:T(8,128)} %collective-permute-done.3.theirs_ref, f32[128,2,8,1024]{3,2,1,0:T(8,128)S(1)} %bitcast.10, f32[1024,1024]{1,0:T(8,128)S(1)} %copy-done.1), custom_call_target="tpu_custom_call" | custom-call | tf_op jit(solution)/shard_map/run_chain/pallas_call | solution.py:27
  145.9 17.5 %all_to_all.27.delta_ref = f32[64,8,128]{2,1,0:T(8,128)S(1)} all-to-all(f32[64,8,128]{2,1,0:T(8,128)S(1)} %broadcast_in_dim.36), channel_id=1, replica_groups=mesh['z'=8,'y'=8,'c'=2,'x'=4] {'z','y'}, dimensions={0} | all-to-all | bytes 524288 | tf_op jit(solution)/shard_map/all_to_all | solution.py:53
  163.4 4.8 %collective-permute-start.4 = (f32[64,8,128]{2,1,0:T(8,128)S(1)}, f32[64,8,128]{2,1,0:T(8,128)S(1)}, u32[]{:S(2)}, u32[]{:S(2)}) collective-permute-start(f32[64,8,128]{2,1,0:T(8,128)S(1)} %all_to_all.27.delta_ref), channel_id=1, source_target_pairs={{0,4},{4,0},{1,5},{5,1},{2,6},{6,2},{3,7},{7,3},{8,12},{12,8},{9,1... | collective-permute-start | bytes 786440 | tf_op jit(solution)/shard_map/ppermute | solution.py:49
  168.2 0.0 copy-done.3
  168.2 0.0 copy-done.5
  168.2 0.0 copy-done.7
  168.3 0.0 copy-done.13
  168.3 2.6 %update.2 = (f32[64,1536]{1,0:T(8,128)S(1)}, f32[64,1536]{1,0:T(8,128)S(1)}) custom-call(s32[2]{0:T(128)S(1)} %copy-done.17, f32[64,8,128]{2,1,0:T(8,128)S(1)} %all_to_all.27.delta_ref, s32[2,1024]{1,0:T(2,128)S(1)} %copy-done.15, f32[64,1536]{1,0:T(8,128)S(1)} %copy-done.12, f32[64,1536]{1,0:T(8,128)S(1)} %copy-done.13, ...), custom_call_target="tpu_custom_call" | custom-call | flops 603979776 | bytes 6291456 | tf_op jit(solution)/shard_map/update/pallas_call | solution.py:27
  170.9 0.0 collective-permute-done.4.delta_ref
  170.9 3.5 %update.3 = (f32[64,1536]{1,0:T(8,128)}, f32[64,1536]{1,0:T(8,128)}) custom-call(s32[2]{0:T(128)S(1)} %copy-done.17, f32[64,8,128]{2,1,0:T(8,128)S(1)} %collective-permute-done.4.delta_ref, s32[2,1024]{1,0:T(2,128)S(1)} %copy-done.15, f32[64,1536]{1,0:T(8,128)S(1)} %get-tuple-element.24.weights_ref, f32[64,1536]{1,0:T(8,128)S(1)} %get-tuple-element.25.fitted_ref, ...), custom_call_target="tpu_custom_call" | custom-call | flops 603979776 | bytes 6291456 | tf_op jit(solution)/shard_map/update/pallas_call | solution.py:27
  (12 shorter events, 0.1 us)
Async XLA Ops:
  7.2 130.6 %all-gather.3.cloned.1.call-start = ((), (), s32[]{:S(2)}) async-start(), calls=%async_computation.5 | async-start | bytes 8454144 | tf_op jit(solution)/shard_map/all_gather | solution.py:392
  7.9 1.3 copy-start.9
  9.2 0.7 copy-start.14
  9.9 0.7 copy-start.16
  10.6 77.1 %copy-start.10 = (bf16[1536,440]{0,1:T(8,128)(2,1)S(1)}, bf16[1536,440]{0,1:T(8,128)(2,1)}, u32[]{:S(2)}) copy-start(bf16[1536,440]{0,1:T(8,128)(2,1)} %param.7) | copy-start | bytes 4055044
  12.0 9.9 %collective-permute-start = (bf16[2,512,128]{2,1,0:T(8,128)(2,1)S(1)}, bf16[2,512,128]{2,1,0:T(8,128)(2,1)S(1)}, u32[]{:S(2)}, u32[]{:S(2)}) collective-permute-start(bf16[2,512,128]{2,1,0:T(8,128)(2,1)S(1)} %get-tuple-element.15), channel_id=1, source_target_pairs={{0,4},{4,0},{1,5},{5,1},{2,6},{6,2},{3,7},{7,3},{8,12},{12,8},{9,1... | collective-permute-start | bytes 786440 | tf_op jit(solution)/shard_map/ppermute | solution.py:49
  22.7 24.8 %all-to-all-start = ((bf16[64,16,128]{2,1,0:T(8,128)(2,1)}), bf16[64,16,128]{2,1,0:T(8,128)(2,1)S(1)}, u32[]{:S(2)}, u32[]{:S(2)}) async-start(bf16[64,16,128]{2,1,0:T(8,128)(2,1)} %bitcast.1), calls=%async_computation | async-start | bytes 524288 | tf_op jit(solution)/shard_map/all_to_all | solution.py:53
  65.4 23.9 %copy-start.12 = (f32[64,1536]{1,0:T(8,128)S(1)}, f32[64,1536]{1,0:T(8,128)}, u32[]{:S(2)}) copy-start(f32[64,1536]{1,0:T(8,128)} %weights_ref.5) | copy-start | bytes 1179652
  65.4 23.9 %copy-start.15 = (s32[2,1024]{1,0:T(2,128)S(1)}, s32[2,1024]{1,0:T(2,128)}, u32[]{:S(2)}) copy-start(s32[2,1024]{1,0:T(2,128)} %index_ref.11) | copy-start | bytes 24580
  65.4 23.9 %copy-start.17 = (s32[2]{0:T(128)S(1)}, s32[2]{0:T(128)}, u32[]{:S(2)}) copy-start(s32[2]{0:T(128)} %owners.13) | copy-start | bytes 28
  81.0 20.3 %collective-permute-start.1 = (bf16[4,1024,128]{2,1,0:T(8,128)(2,1)}, bf16[4,1024,128]{2,1,0:T(8,128)(2,1)}, u32[]{:S(2)}, u32[]{:S(2)}) collective-permute-start(bf16[4,1024,128]{2,1,0:T(8,128)(2,1)} %all_to_all.26.blocks_ref.own_ref), channel_id=1, source_target_pairs={{0,4},{4,0},{1,5},{5,1},{2,6},{6,2},{3,7},{7,3},{8,12},{12,8},{9,1... | collective-permute-start | bytes 3145736 | tf_op jit(solution)/shard_map/ppermute | solution.py:49
  89.3 1.5 copy-start.11
  90.7 1.0 copy-start.18
  97.6 1.6 copy-start.2
  99.2 11.3 %collective-permute-start.2 = (f32[64,8,128]{2,1,0:T(8,128)S(1)}, f32[64,8,128]{2,1,0:T(8,128)S(1)}, u32[]{:S(2)}, u32[]{:S(2)}) collective-permute-start(f32[64,8,128]{2,1,0:T(8,128)S(1)} %get-tuple-element.17), channel_id=1, source_target_pairs={{0,4},{4,0},{1,5},{5,1},{2,6},{6,2},{3,7},{7,3},{8,12},{12,8},{9,1... | collective-permute-start | bytes 786440 | tf_op jit(solution)/shard_map/ppermute | solution.py:49
  107.2 1.7 copy-start.4
  108.8 1.7 copy-start.6
  111.3 21.4 %all-to-all-start.3 = ((f32[64,8,128]{2,1,0:T(8,128)}), f32[64,8,128]{2,1,0:T(8,128)}, u32[]{:S(2)}, u32[]{:S(2)}) async-start(f32[64,8,128]{2,1,0:T(8,128)} %add.7), calls=%async_computation.3 | async-start | bytes 524288 | tf_op jit(solution)/shard_map/all_to_all | solution.py:53
  123.3 2.0 %copy-start = (f32[1024,1024]{1,0:T(8,128)}, f32[1024,1024]{1,0:T(8,128)S(1)}, u32[]{:S(2)}) copy-start(f32[1024,1024]{1,0:T(8,128)S(1)} %between_blocks.1.between_ref) | copy-start | bytes 12582916
  133.7 4.0 %collective-permute-start.3 = (f32[8,128]{1,0:T(8,128)S(1)}, f32[8,128]{1,0:T(8,128)}, u32[]{:S(2)}, u32[]{:S(2)}) collective-permute-start(f32[8,128]{1,0:T(8,128)S(1)} %reduce_sum.9.mine_ref), channel_id=1, source_target_pairs={{0,4},{4,0},{1,5},{5,1},{2,6},{6,2},{3,7},{7,3},{8,12},{12,8},{9,1... | collective-permute-start | bytes 12296 | tf_op jit(solution)/shard_map/ppermute | solution.py:49
  137.8 2.2 %copy-start.1 = (f32[1024,1024]{1,0:T(8,128)S(1)}, f32[1024,1024]{1,0:T(8,128)}, u32[]{:S(2)}) copy-start(f32[1024,1024]{1,0:T(8,128)} %copy-done) | copy-start | bytes 12582916
  140.0 3.4 %copy-start.8 = (f32[256,8,1024]{2,1,0:T(8,128)S(1)}, f32[256,8,1024]{2,1,0:T(8,128)}, u32[]{:S(2)}) copy-start(f32[256,8,1024]{2,1,0:T(8,128)} %all-gather.3.cloned.1.call-done) | copy-start | bytes 25165828
  143.3 24.9 %copy-start.3 = (bf16[4,1536,256]{2,1,0:T(8,128)(2,1)S(1)}, bf16[4,1536,256]{2,1,0:T(8,128)(2,1)}, u32[]{:S(2)}) copy-start(bf16[4,1536,256]{2,1,0:T(8,128)(2,1)} %copy-done.2) | copy-start | bytes 9437188
  143.3 24.9 %copy-start.5 = (bf16[4,1536,256]{2,1,0:T(8,128)(2,1)S(1)}, bf16[4,1536,256]{2,1,0:T(8,128)(2,1)}, u32[]{:S(2)}) copy-start(bf16[4,1536,256]{2,1,0:T(8,128)(2,1)} %copy-done.4) | copy-start | bytes 9437188
  143.3 24.9 %copy-start.7 = (bf16[4,1536,256]{2,1,0:T(8,128)(2,1)S(1)}, bf16[4,1536,256]{2,1,0:T(8,128)(2,1)}, u32[]{:S(2)}) copy-start(bf16[4,1536,256]{2,1,0:T(8,128)(2,1)} %copy-done.6) | copy-start | bytes 9437188
  143.3 24.9 %copy-start.13 = (f32[64,1536]{1,0:T(8,128)S(1)}, f32[64,1536]{1,0:T(8,128)}, u32[]{:S(2)}) copy-start(f32[64,1536]{1,0:T(8,128)} %fitted_ref.1) | copy-start | bytes 1179652
  163.4 7.5 %collective-permute-start.4 = (f32[64,8,128]{2,1,0:T(8,128)S(1)}, f32[64,8,128]{2,1,0:T(8,128)S(1)}, u32[]{:S(2)}, u32[]{:S(2)}) collective-permute-start(f32[64,8,128]{2,1,0:T(8,128)S(1)} %all_to_all.27.delta_ref), channel_id=1, source_target_pairs={{0,4},{4,0},{1,5},{5,1},{2,6},{6,2},{3,7},{7,3},{8,12},{12,8},{9,1... | collective-permute-start | bytes 786440 | tf_op jit(solution)/shard_map/ppermute | solution.py:49
Sparse Core Ops, SparseCore 0:
  11.1 98.3 all-gather.2

commit v3 on v2

--- a/solution.py
+++ b/solution.py
@@ -23,7 +23,15 @@
 WHOLE = pl.BlockSpec(memory_space=pltpu.VMEM)
 
 
-def call(kernel, name, shapes, owners, *args, scratch=(), aliases=None, cost=None):
+def call(
+    kernel,
+    name,
+    shapes,
+    owners,
+    *args,
+    scratch=(),
+    cost=None,
+):
     return pl.pallas_call(
         kernel,
         grid_spec=pltpu.PrefetchScalarGridSpec(
@@ -34,7 +42,6 @@
             scratch_shapes=list(scratch),
         ),
         out_shape=[jax.ShapeDtypeStruct(*shape) for shape in shapes],
-        input_output_aliases=aliases or {},
         compiler_params=pltpu.CompilerParams(vmem_limit_bytes=VMEM_BYTES),
         cost_estimate=cost,
         name=name,
@@ -69,6 +76,12 @@
     return lax.dot_general(left, right, dims, preferred_element_type=F32)
 
 
+def exact_dot(value, pick, dims=(((1,), (0,)), ((), ()))):
+    rows = value.shape[0]
+    terms = dot(jnp.concatenate(three_parts(value), axis=0), pick, dims)
+    return terms[:rows] + (terms[rows : 2 * rows] + terms[2 * rows :])
+
+
 def one_hot(count, numbers):
     rows = lax.broadcasted_iota(jnp.int32, (count, numbers.shape[1]), 0)
     return jnp.where(rows == numbers, 1.0, 0.0).astype(BF16)
@@ -80,7 +93,7 @@
     return jnp.where(step == 0, tiles[0:1], tiles[1:2])
 
 
-def pick_kernel(owners, points_ref, index_ref, keep_ref, send_ref):
+def pick_kernel(points_ref, index_ref, keep_ref, send_ref):
     features, count = points_ref.shape
     steps = index_ref.shape[0]
     core, line = lax.axis_index("c"), lax.axis_index("x")
@@ -98,15 +111,67 @@
             ref[step] = picked[:, at : at + LANES]
 
 
-def pick_blocks(owners, points, index):
-    shape = ((index.shape[0], FEATURE_ROWS, LANES), BF16)
-    return call(pick_kernel, "pick_blocks", [shape, shape], owners, points.T, index)
-
-
-def kernel_kernel(
+def pick_blocks(points, index):
+    shape = jax.ShapeDtypeStruct((index.shape[0], FEATURE_ROWS, LANES), BF16)
+    block = pl.BlockSpec(shape.shape, lambda i: (0, 0, 0))
+    return pl.pallas_call(
+        pick_kernel,
+        grid=(1,),
+        in_specs=[pl.BlockSpec(array.shape, lambda i: (0, 0)) for array in (points, index)],
+        out_specs=[block, block],
+        out_shape=[shape, shape],
+        compiler_params=pltpu.CompilerParams(vmem_limit_bytes=VMEM_BYTES),
+        name="pick_blocks",
+    )(points, index)
+
+
+def choose_kernel(owners, keep_ref, got_ref, out_ref):
+    core = lax.axis_index("c")
+    for step in range(out_ref.shape[0]):
+        mine = (owners[step] & 1) == core
+        out_ref[step] = jnp.where(mine, keep_ref[step], got_ref[step])
+
+
+def choose(owners, keep, got):
+    return call(choose_kernel, "choose", [(keep.shape, BF16)], owners, keep, got)[0]
+
+
+def take_kernel(owners, parcels_ref, out_ref):
+    groups = parcels_ref.shape[0]
+    per_step = groups // owners.shape[0]
+    zy = lax.axis_index("z") * GRID[1] + lax.axis_index("y")
+    holder = jnp.where(zy < per_step, owners[0], owners[1]) >> 1
+    piece = parcels_ref[pl.ds(holder, 1)]
+    out_ref[...] = jnp.broadcast_to(piece, out_ref.shape)
+
+
+def take(owners, parcels):
+    return call(take_kernel, "take", [(parcels.shape, BF16)], owners, parcels)[0]
+
+
+def prepare(features, points_ref, weights_ref, rows_ref, norms_ref, parts_ref):
+    count = points_ref.shape[1]
+    outs = weights_ref.shape[0]
+    gamma = 2.0 / features
+    empty = jnp.zeros((FEATURE_ROWS - features, LANES), F32)
+    for at in range(0, count, LANES):
+        rows = slice(at, at + LANES)
+        wide = jnp.concatenate([points_ref[:, rows].astype(F32), empty], axis=0)
+        wide = jnp.transpose(wide)
+        rows_ref[rows, :] = wide.astype(BF16)
+        norms_ref[rows, :] = gamma * jnp.sum(wide * wide, axis=1, keepdims=True)
+    high, low = two_parts(weights_ref[...])
+    parts_ref[:outs, :] = high
+    parts_ref[outs:, :] = low
+
+
+def kernel_body(
+    features,
     foreign,
     owners,
-    points_ref,
+    rows_ref,
+    norms_ref,
+    parts_ref,
     weights_ref,
     targets_ref,
     index_ref,
@@ -114,20 +179,12 @@
     grad_ref,
     high_ref,
     low_ref,
-    parts,
-    norms,
 ):
-    count, features = points_ref.shape
+    count = rows_ref.shape[0]
     outs = weights_ref.shape[0]
     pairs = blocks_ref.shape[0] // 2
     steps = index_ref.shape[0]
     gamma = 2.0 / features
-    high, low = two_parts(weights_ref[...])
-    parts[:outs, :] = high
-    parts[outs:, :] = low
-    for at in range(0, count, CHUNK):
-        wide = points_ref[at : at + CHUNK, :].astype(F32)
-        norms[at : at + CHUNK, :] = gamma * jnp.sum(wide * wide, axis=1, keepdims=True)
 
     blocks, block_norms, grads = [], [], []
     for step in range(steps):
@@ -137,14 +194,14 @@
                 [blocks_ref[2 * pair, rows, :], blocks_ref[2 * pair + 1, rows, :]], axis=1
             )
             wide = block.astype(F32)
-            blocks.append(block[:features, :])
+            blocks.append(block)
             block_norms.append(gamma * jnp.sum(wide * wide, axis=0, keepdims=True))
             grads.append(jnp.zeros((outs, 2 * LANES), F32))
 
     units = [(n, at) for n in range(steps * pairs) for at in range(0, count, UNIT)]
 
     def cross(n, at):
-        return dot(points_ref[at : at + UNIT, :], blocks[n])
+        return dot(rows_ref[at : at + UNIT, :], blocks[n])
 
     ahead = cross(*units[0])
     for place, (n, at) in enumerate(units):
@@ -152,19 +209,16 @@
         if place + 1 < len(units):
             ahead = cross(*units[place + 1])
         rows = slice(at, at + UNIT)
-        kern = jnp.exp((2.0 * gamma) * now - (norms[rows, :] + block_norms[n]))
+        kern = jnp.exp((2.0 * gamma) * now - (norms_ref[rows, :] + block_norms[n]))
         high, low = two_parts(kern)
         high_ref[n, rows, :] = high
         low_ref[n, rows, :] = low
-        both = dot(parts[:, rows], high)
-        grads[n] += both[:outs] + both[outs:] + dot(parts[:outs, rows], low)
-
-    def tiles(n):
-        step, pair = divmod(n, pairs)
-        return [(step * pairs + pair) * 2 + k for k in range(2)]
+        both = dot(parts_ref[:, rows], high)
+        grads[n] += both[:outs] + both[outs:] + dot(parts_ref[:outs, rows], low)
 
     for n, grad in enumerate(grads):
-        for k, tile in enumerate(tiles(n)):
+        for k in range(2):
+            tile = 2 * n + k
             part = grad[:, k * LANES : (k + 1) * LANES]
             grad_ref[:, tile : tile + 1, :] = part.reshape(outs, 1, LANES)
 
@@ -174,32 +228,46 @@
 
         @pl.when(owners[step] == rank)
         def _():
-            own = three_parts(LAMBDA * weights_ref[...] - targets_ref[...])
-            for line in range(2 * pairs):
-                pick = one_hot(count, index_tile(index_ref, step, line, kind))
-                terms = [dot(part, pick) for part in own]
-                tile = step * 2 * pairs + line
-                grad_ref[:, tile : tile + 1, :] += (
-                    terms[0] + (terms[1] + terms[2])
-                ).reshape(outs, 1, LANES)
-
-
-def kernel_and_gradient(foreign, owners, points, weights, targets, index, blocks):
-    count = points.shape[0]
-    outs = weights.shape[0]
+            own = LAMBDA * weights_ref[...] - targets_ref[...]
+            for pair in range(pairs):
+                numbers = [index_tile(index_ref, step, 2 * pair + k, kind) for k in range(2)]
+                term = exact_dot(own, one_hot(count, jnp.concatenate(numbers, axis=1)))
+                for k in range(2):
+                    tile = (step * pairs + pair) * 2 + k
+                    part = term[:, k * LANES : (k + 1) * LANES]
+                    grad_ref[:, tile : tile + 1, :] += part.reshape(outs, 1, LANES)
+
+
+def first_kernel(features, owners, points, weights, targets, index, blocks, *rest):
+    grad, high, low, rows, norms, parts = rest
+    prepare(features, points, weights, rows, norms, parts)
+    kernel_body(
+        features, 0, owners, rows, norms, parts, weights, targets, index, blocks,
+        grad, high, low,
+    )
+
+
+def second_kernel(features, *refs):
+    kernel_body(features, 1, *refs)
+
+
+def kernel_and_gradient(features, owners, data, weights, targets, index, blocks, first):
+    outs, count = weights.shape
     tiles = index.shape[0] * blocks.shape[0]
-    kern = ((tiles // 2, count, 2 * LANES), BF16)
+    kern = (tiles // 2, count, 2 * LANES)
+    shapes = [((outs, tiles, LANES), F32), (kern, BF16), (kern, BF16)]
+    if first:
+        shapes += [((count, FEATURE_ROWS), BF16), ((count, 1), F32), ((2 * outs, count), BF16)]
     return call(
-        functools.partial(kernel_kernel, foreign),
-        "kernel_and_gradient",
-        [((outs, tiles, LANES), F32), kern, kern],
+        functools.partial(first_kernel if first else second_kernel, features),
+        "first_half" if first else "second_half",
+        shapes,
         owners,
-        points,
+        *data,
         weights,
         targets,
         index,
         blocks,
-        scratch=[pltpu.VMEM((2 * outs, count), BF16), pltpu.VMEM((count, 1), F32)],
         cost=pl.CostEstimate(
             flops=tiles * LANES * count * (2 * FEATURE_ROWS + 6 * outs),
             bytes_accessed=4 * tiles * LANES * count,
@@ -260,7 +328,7 @@
 
 
 def chain_kernel(owners, mine_ref, theirs_ref, given_ref, between_ref, out_ref, grads):
-    tiles = out_ref.shape[1]
+    tiles = out_ref.shape[0]
     block = between_ref.shape[0]
     rows = given_ref.shape[2]
     lines = tiles // 2
@@ -287,7 +355,10 @@
             given = given_ref[n * share : (n + 1) * share, step].reshape(LANES, block)
             delta = jnp.sum(given * grad, axis=1, keepdims=True)
             row = jnp.sum(jnp.where(diagonal, delta, 0.0), axis=0, keepdims=True)
-            out_ref[step, n : n + 1, :] = row
+            if step == 0:
+                out_ref[n : n + 1, :] = row
+            else:
+                out_ref[n : n + 1, :] = jnp.where(core == 0, out_ref[n : n + 1, :], row)
             if step == 0:
                 product = delta * between_ref[n * LANES : (n + 1) * LANES, :]
                 correction += jnp.sum(product.reshape(-1, 8, block), axis=0)
@@ -298,7 +369,7 @@
     return call(
         chain_kernel,
         "run_chain",
-        [((2, block // LANES, LANES), F32)],
+        [((block // LANES, LANES), F32)],
         owners,
         mine,
         theirs,
@@ -356,8 +427,7 @@
         for pair, kind, delta in deltas:
             numbers = [index_tile(index_ref, step, 2 * pair + k, kind) for k in range(2)]
             pick = one_hot(count, jnp.concatenate(numbers, axis=1))
-            terms = [dot(part, pick, TRANSPOSED) for part in three_parts(delta)]
-            new_weights_ref[...] -= terms[0] + (terms[1] + terms[2])
+            new_weights_ref[...] -= exact_dot(delta, pick, TRANSPOSED)
 
 
 def update(foreign, owners, delta, index, weights, fitted, own, other):
@@ -386,37 +456,32 @@
     features = points.shape[1]
     groups = GRID[0] * GRID[1]
     lines = lax.axis_size("x")
-    core = lax.axis_index("c")
-    per_step = (groups // steps).bit_length() - 1
 
     given = lax.all_gather(preconditioner, DP, axis=0)
 
-    keep, send = pick_blocks(owners, points, block_index)
-    got = exchange(send)
-    owner_core = (owners & 1).reshape(steps, 1, 1)
-    parcels = jnp.where(owner_core == core, keep, got)
-    parcels = all_to_all(parcels.reshape(groups, -1, LANES), ZY)
-    late = lax.axis_index(ZY) >> per_step
-    holder = (jnp.where(late == 0, owners[0], owners[1]) >> 1).astype(jnp.uint32)
-    zero = jnp.uint32(0)
-    piece = lax.dynamic_slice(parcels, (holder, zero, zero), (1, *parcels.shape[1:]))
-    blocks = all_to_all(jnp.broadcast_to(piece, parcels.shape), ZY)
+    keep, send = pick_blocks(points.T, block_index)
+    parcels = choose(owners, keep, exchange(send)).reshape(groups, -1, LANES)
+    blocks = all_to_all(take(owners, all_to_all(parcels, ZY)), ZY)
     blocks = blocks.reshape(1, steps * FEATURE_ROWS, LANES)
     own = all_to_all(jnp.broadcast_to(blocks, (lines, *blocks.shape[1:])), "x")
     other = exchange(own)
 
-    data = (points, weights, targets, block_index)
-    grad_own, *kern_own = kernel_and_gradient(0, owners, *data, own)
+    data = (weights, targets, block_index)
+    grad_own, *kern_own, rows, norms, parts = kernel_and_gradient(
+        features, owners, (points.T,), *data, own, True
+    )
     grad_theirs = exchange(grad_own)
-    grad_other, *kern_other = kernel_and_gradient(1, owners, *data, other)
+    grad_other, *kern_other = kernel_and_gradient(
+        features, owners, (rows, norms, parts), *data, other, False
+    )
     grad = all_to_all(grad_other + grad_theirs, ZY)
+    grad, given, own, other = lax.optimization_barrier((grad, given, own, other))
     grad = jnp.sum(grad, axis=0)
+    theirs = exchange(grad)
     between = between_blocks(features, owners, block_index, own, other)
-    grad, between = lax.optimization_barrier((grad, between))
-    delta = run_chain(owners, grad, exchange(grad), given, between)
-
-    mine = jnp.where(core == 0, delta[0], delta[1])[None]
-    mine = all_to_all(jnp.broadcast_to(mine, (groups, *mine.shape[1:])), ZY)
+    mine = run_chain(owners, grad, theirs, given, between)
+
+    mine = all_to_all(jnp.broadcast_to(mine, (groups, *mine.shape)), ZY)
     theirs = exchange(mine)
     rest = (kern_own, kern_other)
     weights, fitted = update(0, owners, mine, block_index, weights, fitted, *rest)

time: 182 us -> 176 us (0.967)
  blocking collectives: 50.8 us -> 94.4 us
  waiting for transfers between devices: 20.8 us -> 1.83 us
  starting transfers between devices: 43.9 us -> 26.6 us
  local copies, waits for them, and re-layouts: 20.8 us -> 14.5 us
  Pallas kernels: 26.2 us -> 22.2 us
  other arithmetic: 3.21 us -> 1.05 us
    all_to_all x3 -> x5, blocking collectives: 50.8 us -> 94.4 us  [all_to_all(): return lax.all_to_all(value, axes, 0, 0, tiled=True)]
    all_to_all x2 -> x0, waiting for transfers between devices: 18.7 us -> none  [all_to_all(): return lax.all_to_all(value, axes, 0, 0, tiled=True)]
    all_to_all x2 -> x0, starting transfers between devices: 18.4 us -> none  [all_to_all(): return lax.all_to_all(value, axes, 0, 0, tiled=True)]
    unnamed x39 -> x42, local copies, waits for them, and re-layouts: 19.3 us -> 14.3 us
    pallas_call x7 -> x8, Pallas kernels: 26.2 us -> 21.4 us  [call(): pl.pallas_call(kernel, grid_spec=pltpu.PrefetchScalarGridSpec(num_scalar_...]
  transfers between devices with their start and end apart: 8 -> 6, of which waited for: 4 -> 1; matrix products, arithmetic and copies ran while one was open for 3% -> 0% of each run, Pallas kernels for 11% -> 10%
where the time goes in v3:
time: 176 us; the launch traced here: 175 us
  blocking collectives  94.4 us (54%)
  starting transfers between devices  26.6 us (15%)
  Pallas kernels  22.2 us (13%)
  local copies, waits for them, and re-layouts  14.5 us (8%)
  between operations  14.3 us (8%)
  waiting for transfers between devices  1.83 us (1%)
    all_to_all x5, blocking collectives, all_to_all(): return lax.all_to_all(value, axes, 0, 0, tiled=True)  94.4 us
    ppermute x5, starting transfers between devices, exchange(): return lax.ppermute(value, 'c', [(0, 1), (1, 0)])  26.5 us
    pallas_call x8, Pallas kernels, call(): pl.pallas_call(kernel, grid_spec=pltpu.PrefetchScalarGridSpec(num_scalar_...  21.4 us
    unnamed x42, local copies, waits for them, and re-layouts  14.3 us
  transfers between devices with their start and end apart: 6, of which 1 were waited for; matrix products, arithmetic and copies ran while one was open for 0% of the time, Pallas kernels for 10%

profile of v3, /device:TPU:1, one launch (start us, length us, event | category | flops | bytes accessed | tf_op | source)
XLA Modules:
  0.0 174.9 jit_solution(7254463790996822521)
XLA Ops:
  7.2 0.0 all-gather.3.cloned.1.call-start
  7.2 0.7 all-gather.3.cloned.1.call-update
  7.9 0.0 copy-start.9
  7.9 1.3 copy-done.9
  9.2 0.0 copy-start.15
  9.2 0.7 copy-done.15
  9.9 0.0 copy-start.20
  9.9 0.9 pick_blocks.1
  10.8 0.0 copy-start.10
  10.8 0.0 copy-start.13
  10.8 8.9 %collective-permute-start = (bf16[2,512,128]{2,1,0:T(8,128)(2,1)S(1)}, bf16[2,512,128]{2,1,0:T(8,128)(2,1)S(1)}, u32[]{:S(2)}, u32[]{:S(2)}) collective-permute-start(bf16[2,512,128]{2,1,0:T(8,128)(2,1)S(1)} %get-tuple-element.20), channel_id=1, source_target_pairs={{0,4},{4,0},{1,5},{5,1},{2,6},{6,2},{3,7},{7,3},{8,12},{12,8},{9,1... | collective-permute-start | bytes 786440 | tf_op jit(solution)/shard_map/ppermute | solution.py:56
  19.8 1.1 collective-permute-done.got_ref
  20.9 0.7 copy-done.17
  21.6 0.6 choose.1
  22.2 24.8 %all_to_all.25.parcels_ref = bf16[64,16,128]{2,1,0:T(8,128)(2,1)S(1)} all-to-all(bf16[64,16,128]{2,1,0:T(8,128)(2,1)S(1)} %bitcast.7), channel_id=1, replica_groups=mesh['z'=8,'y'=8,'c'=2,'x'=4] {'z','y'}, dimensions={0} | all-to-all | bytes 524288 | tf_op jit(solution)/shard_map/all_to_all | solution.py:60
  47.0 0.0 copy-start.18
  47.0 0.7 copy-done.18
  47.6 0.6 take.1
  48.2 17.6 %all_to_all.26 = bf16[64,16,128]{2,1,0:T(8,128)(2,1)S(1)} all-to-all(bf16[64,16,128]{2,1,0:T(8,128)(2,1)S(1)} %take.1), channel_id=1, replica_groups=mesh['z'=8,'y'=8,'c'=2,'x'=4] {'z','y'}, dimensions={0} | all-to-all | bytes 524288 | tf_op jit(solution)/shard_map/all_to_all | solution.py:60
  65.8 0.1 broadcast_in_dim.11
  66.0 15.2 %all_to_all.27.blocks.own_ref = bf16[4,1024,128]{2,1,0:T(8,128)(2,1)S(1)} all-to-all(bf16[4,1024,128]{2,1,0:T(8,128)(2,1)S(1)} %broadcast_in_dim.11), channel_id=1, replica_groups=mesh['z'=8,'y'=8,'c'=2,'x'=4] {'x'}, dimensions={0} | all-to-all | bytes 2097152 | tf_op jit(solution)/shard_map/all_to_all | solution.py:60
  81.1 6.7 %collective-permute-start.1 = (bf16[4,1024,128]{2,1,0:T(8,128)(2,1)S(1)}, bf16[4,1024,128]{2,1,0:T(8,128)(2,1)S(1)}, u32[]{:S(2)}, u32[]{:S(2)}) collective-permute-start(bf16[4,1024,128]{2,1,0:T(8,128)(2,1)S(1)} %all_to_all.27.blocks.own_ref), channel_id=1, source_target_pairs={{0,4},{4,0},{1,5},{5,1},{2,6},{6,2},{3,7},{7,3},{8,12},{12,8},{9,1... | collective-permute-start | bytes 3145736 | tf_op jit(solution)/shard_map/ppermute | solution.py:56
  87.9 0.0 copy-done.20
  87.9 0.0 copy-done.10
  87.9 0.0 copy-done.13
  87.9 5.1 %first_half.1 = (f32[64,8,128]{2,1,0:T(8,128)S(1)}, bf16[4,1536,256]{2,1,0:T(8,128)(2,1)S(1)}, bf16[4,1536,256]{2,1,0:T(8,128)(2,1)S(1)}, bf16[1536,512]{1,0:T(8...) custom-call(s32[2]{0:T(128)S(1)} %copy-done.18, bf16[440,1536]{1,0:T(8,128)(2,1)S(1)} %bitcast.6, ...), custom_call_target="tpu_custom_call" | custom-call | flops 2214592512 | bytes 6291456 | tf_op jit(solution)/shard_map/first_half/pallas_call | solution.py:35
  93.0 0.0 copy-done.7
  93.0 0.0 copy-start
  93.0 1.6 copy-done
  94.6 2.1 %collective-permute-start.2 = (f32[64,8,128]{2,1,0:T(8,128)S(1)}, f32[64,8,128]{2,1,0:T(8,128)S(1)}, u32[]{:S(2)}, u32[]{:S(2)}) collective-permute-start(f32[64,8,128]{2,1,0:T(8,128)S(1)} %get-tuple-element.25), channel_id=1, source_target_pairs={{0,4},{4,0},{1,5},{5,1},{2,6},{6,2},{3,7},{7,3},{8,12},{12,8},{9,1... | collective-permute-start | bytes 786440 | tf_op jit(solution)/shard_map/ppermute | solution.py:56
  96.7 0.0 collective-permute-done.1.refs_7_.other_ref
  96.8 0.0 copy-start.11
  96.8 0.0 copy-done.16
  96.8 0.0 copy-start.19
  96.8 4.5 %second_half.1 = (f32[64,8,128]{2,1,0:T(8,128)S(1)}, bf16[4,1536,256]{2,1,0:T(8,128)(2,1)S(1)}, bf16[4,1536,256]{2,1,0:T(8,128)(2,1)S(1)}) custom-call(s32[2]{0:T(128)S(1)} %copy-done.18, bf16[1536,512]{1,0:T(8,128)(2,1)S(1)} %get-tuple-element.21.refs_1_, f32[1536,1]{1,0:T(8,128)S(1)} %get-tuple-element.22.refs_2_, ...), custom_call_target="tpu_custom_call" | custom-call | flops 2214592512 | bytes 6291456 | tf_op jit(solution)/shard_map/second_half/pallas_call | solution.py:35
  101.3 0.0 copy-done.11
  101.3 0.0 copy-start.2
  101.3 1.7 copy-done.2
  103.0 1.6 copy-done.4
  104.7 0.0 collective-permute-done.2
  104.7 19.2 %all_to_all.28 = f32[64,8,128]{2,1,0:T(8,128)} all-to-all(f32[64,8,128]{2,1,0:T(8,128)S(1)} %add.3), channel_id=1, replica_groups=mesh['z'=8,'y'=8,'c'=2,'x'=4] {'z','y'}, dimensions={0} | all-to-all | bytes 524288 | tf_op jit(solution)/shard_map/all_to_all | solution.py:60
  123.9 1.0 reduce_sum.9.mine_ref
  124.9 4.8 %collective-permute-start.3 = (f32[8,128]{1,0:T(8,128)S(1)}, f32[8,128]{1,0:T(8,128)S(1)}, u32[]{:S(2)}, u32[]{:S(2)}) collective-permute-start(f32[8,128]{1,0:T(8,128)S(1)} %reduce_sum.9.mine_ref), channel_id=1, source_target_pairs={{0,4},{4,0},{1,5},{5,1},{2,6},{6,2},{3,7},{7,3},{8,12},{12,8},{9,1... | collective-permute-start | bytes 12296 | tf_op jit(solution)/shard_map/ppermute | solution.py:56
  129.7 0.0 copy-done.19
  129.7 0.0 copy-start.8
  129.8 1.2 copy-done.8
  131.0 1.2 copy-done.12
  132.2 2.9 %between_blocks.1.between_ref = f32[1024,1024]{1,0:T(8,128)S(1)} custom-call(s32[2]{0:T(128)S(1)} %copy-done.19, s32[2,1024]{1,0:T(2,128)S(1)} %copy-done.16, bf16[4,1024,128]{2,1,0:T(8,128)(2,1)S(1)} %copy-done.8, bf16[4,1024,128]{2,1,0:T(8,128)(2,1)S(1)} %copy-done.12), custom_call_target="tpu_custom_call" | custom-call | flops 1073741824 | bytes 4194304 | tf_op jit(solution)/shard_map/between_blocks/pallas_call | solution.py:35
  135.1 0.0 copy-start.1
  135.2 0.0 copy-start.3
  135.2 0.0 copy-start.5
  135.2 0.0 collective-permute-done.3.theirs_ref
  135.2 0.0 copy-start.6
  135.2 3.5 %copy-done.6 = f32[256,8,1024]{2,1,0:T(8,128)S(1)} copy-done((f32[256,8,1024]{2,1,0:T(8,128)S(1)}, f32[256,8,1024]{2,1,0:T(8,128)}, u32[]{:S(2)}) %copy-start.6) | copy-done | bytes 8388632
  138.7 1.5 run_chain.1
  140.2 17.7 %all_to_all.29.delta_ref = f32[64,8,128]{2,1,0:T(8,128)S(1)} all-to-all(f32[64,8,128]{2,1,0:T(8,128)S(1)} %broadcast_in_dim.12), channel_id=1, replica_groups=mesh['z'=8,'y'=8,'c'=2,'x'=4] {'z','y'}, dimensions={0} | all-to-all | bytes 524288 | tf_op jit(solution)/shard_map/all_to_all | solution.py:60
  157.9 3.9 %collective-permute-start.4 = (f32[64,8,128]{2,1,0:T(8,128)S(1)}, f32[64,8,128]{2,1,0:T(8,128)S(1)}, u32[]{:S(2)}, u32[]{:S(2)}) collective-permute-start(f32[64,8,128]{2,1,0:T(8,128)S(1)} %all_to_all.29.delta_ref), channel_id=1, source_target_pairs={{0,4},{4,0},{1,5},{5,1},{2,6},{6,2},{3,7},{7,3},{8,12},{12,8},{9,1... | collective-permute-start | bytes 786440 | tf_op jit(solution)/shard_map/ppermute | solution.py:56
  161.9 0.0 copy-done.1
  161.9 0.0 copy-done.3
  161.9 0.0 copy-done.5
  161.9 0.0 copy-done.14
  161.9 2.6 %update.2 = (f32[64,1536]{1,0:T(8,128)S(1)}, f32[64,1536]{1,0:T(8,128)S(1)}) custom-call(s32[2]{0:T(128)S(1)} %copy-done.19, f32[64,8,128]{2,1,0:T(8,128)S(1)} %all_to_all.29.delta_ref, s32[2,1024]{1,0:T(2,128)S(1)} %copy-done.16, f32[64,1536]{1,0:T(8,128)S(1)} %copy-done.13, f32[64,1536]{1,0:T(8,128)S(1)} %copy-done.14, ...), custom_call_target="tpu_custom_call" | custom-call | flops 603979776 | bytes 6291456 | tf_op jit(solution)/shard_map/update/pallas_call | solution.py:35
  164.5 0.0 collective-permute-done.4.delta_ref
  164.5 3.5 %update.3 = (f32[64,1536]{1,0:T(8,128)}, f32[64,1536]{1,0:T(8,128)}) custom-call(s32[2]{0:T(128)S(1)} %copy-done.19, f32[64,8,128]{2,1,0:T(8,128)S(1)} %collective-permute-done.4.delta_ref, s32[2,1024]{1,0:T(2,128)S(1)} %copy-done.16, f32[64,1536]{1,0:T(8,128)S(1)} %get-tuple-element.34.weights_ref, f32[64,1536]{1,0:T(8,128)S(1)} %get-tuple-element.35.fitted_ref, ...), custom_call_target="tpu_custom_call" | custom-call | flops 603979776 | bytes 6291456 | tf_op jit(solution)/shard_map/update/pallas_call | solution.py:35
  (9 shorter events, 0.1 us)
Async XLA Ops:
  7.2 116.7 %all-gather.3.cloned.1.call-start = ((), (), s32[]{:S(2)}) async-start(), calls=%async_computation.5 | async-start | bytes 8454144 | tf_op jit(solution)/shard_map/all_gather | solution.py:460
  7.9 1.3 copy-start.9
  9.2 0.7 copy-start.15
  9.9 78.0 %copy-start.20 = (f32[64,1536]{1,0:T(8,128)S(1)}, f32[64,1536]{1,0:T(8,128)}, u32[]{:S(2)}) copy-start(f32[64,1536]{1,0:T(8,128)} %refs_5_.1) | copy-start | bytes 1179652
  10.8 77.1 %copy-start.10 = (bf16[1536,440]{0,1:T(8,128)(2,1)S(1)}, bf16[1536,440]{0,1:T(8,128)(2,1)}, u32[]{:S(2)}) copy-start(bf16[1536,440]{0,1:T(8,128)(2,1)} %param.7) | copy-start | bytes 4055044
  10.8 77.1 %copy-start.13 = (f32[64,1536]{1,0:T(8,128)S(1)}, f32[64,1536]{1,0:T(8,128)}, u32[]{:S(2)}) copy-start(f32[64,1536]{1,0:T(8,128)} %weights_ref.1) | copy-start | bytes 1179652
  10.8 10.1 %collective-permute-start = (bf16[2,512,128]{2,1,0:T(8,128)(2,1)S(1)}, bf16[2,512,128]{2,1,0:T(8,128)(2,1)S(1)}, u32[]{:S(2)}, u32[]{:S(2)}) collective-permute-start(bf16[2,512,128]{2,1,0:T(8,128)(2,1)S(1)} %get-tuple-element.20), channel_id=1, source_target_pairs={{0,4},{4,0},{1,5},{5,1},{2,6},{6,2},{3,7},{7,3},{8,12},{12,8},{9,1... | collective-permute-start | bytes 786440 | tf_op jit(solution)/shard_map/ppermute | solution.py:56
  20.9 0.7 copy-start.17
  47.0 0.7 copy-start.18
  81.1 11.8 %copy-start.7 = (bf16[4,1024,128]{2,1,0:T(8,128)(2,1)}, bf16[4,1024,128]{2,1,0:T(8,128)(2,1)S(1)}, u32[]{:S(2)}) copy-start(bf16[4,1024,128]{2,1,0:T(8,128)(2,1)S(1)} %all_to_all.27.blocks.own_ref) | copy-start | bytes 3145732
  81.1 15.6 %copy-start.16 = (s32[2,1024]{1,0:T(2,128)S(1)}, s32[2,1024]{1,0:T(2,128)}, u32[]{:S(2)}) copy-start(s32[2,1024]{1,0:T(2,128)} %index_ref.7) | copy-start | bytes 24580
  81.1 15.6 %collective-permute-start.1 = (bf16[4,1024,128]{2,1,0:T(8,128)(2,1)S(1)}, bf16[4,1024,128]{2,1,0:T(8,128)(2,1)S(1)}, u32[]{:S(2)}, u32[]{:S(2)}) collective-permute-start(bf16[4,1024,128]{2,1,0:T(8,128)(2,1)S(1)} %all_to_all.27.blocks.own_ref), channel_id=1, source_target_pairs={{0,4},{4,0},{1,5},{5,1},{2,6},{6,2},{3,7},{7,3},{8,12},{12,8},{9,1... | collective-permute-start | bytes 3145736 | tf_op jit(solution)/shard_map/ppermute | solution.py:56
  93.0 1.7 copy-start
  94.6 10.0 %collective-permute-start.2 = (f32[64,8,128]{2,1,0:T(8,128)S(1)}, f32[64,8,128]{2,1,0:T(8,128)S(1)}, u32[]{:S(2)}, u32[]{:S(2)}) collective-permute-start(f32[64,8,128]{2,1,0:T(8,128)S(1)} %get-tuple-element.25), channel_id=1, source_target_pairs={{0,4},{4,0},{1,5},{5,1},{2,6},{6,2},{3,7},{7,3},{8,12},{12,8},{9,1... | collective-permute-start | bytes 786440 | tf_op jit(solution)/shard_map/ppermute | solution.py:56
  96.8 4.6 %copy-start.11 = (bf16[4,1024,128]{2,1,0:T(8,128)(2,1)}, bf16[4,1024,128]{2,1,0:T(8,128)(2,1)S(1)}, u32[]{:S(2)}) copy-start(bf16[4,1024,128]{2,1,0:T(8,128)(2,1)S(1)} %collective-permute-done.1.refs_7_.other_ref) | copy-start | bytes 3145732
  96.8 33.0 %copy-start.19 = (s32[2]{0:T(128)S(1)}, s32[2]{0:T(128)}, u32[]{:S(2)}) copy-start(s32[2]{0:T(128)} %owners.13) | copy-start | bytes 28
  101.3 1.7 copy-start.2
  103.0 1.6 copy-start.4
  124.9 10.3 %collective-permute-start.3 = (f32[8,128]{1,0:T(8,128)S(1)}, f32[8,128]{1,0:T(8,128)S(1)}, u32[]{:S(2)}, u32[]{:S(2)}) collective-permute-start(f32[8,128]{1,0:T(8,128)S(1)} %reduce_sum.9.mine_ref), channel_id=1, source_target_pairs={{0,4},{4,0},{1,5},{5,1},{2,6},{6,2},{3,7},{7,3},{8,12},{12,8},{9,1... | collective-permute-start | bytes 12296 | tf_op jit(solution)/shard_map/ppermute | solution.py:56
  129.7 1.2 copy-start.8
  131.0 1.2 copy-start.12
  135.1 26.7 %copy-start.1 = (bf16[4,1536,256]{2,1,0:T(8,128)(2,1)S(1)}, bf16[4,1536,256]{2,1,0:T(8,128)(2,1)}, u32[]{:S(2)}) copy-start(bf16[4,1536,256]{2,1,0:T(8,128)(2,1)} %copy-done) | copy-start | bytes 9437188
  135.2 26.7 %copy-start.3 = (bf16[4,1536,256]{2,1,0:T(8,128)(2,1)S(1)}, bf16[4,1536,256]{2,1,0:T(8,128)(2,1)}, u32[]{:S(2)}) copy-start(bf16[4,1536,256]{2,1,0:T(8,128)(2,1)} %copy-done.2) | copy-start | bytes 9437188
  135.2 26.7 %copy-start.5 = (bf16[4,1536,256]{2,1,0:T(8,128)(2,1)S(1)}, bf16[4,1536,256]{2,1,0:T(8,128)(2,1)}, u32[]{:S(2)}) copy-start(bf16[4,1536,256]{2,1,0:T(8,128)(2,1)} %copy-done.4) | copy-start | bytes 9437188
  135.2 3.5 %copy-start.6 = (f32[256,8,1024]{2,1,0:T(8,128)S(1)}, f32[256,8,1024]{2,1,0:T(8,128)}, u32[]{:S(2)}) copy-start(f32[256,8,1024]{2,1,0:T(8,128)} %all-gather.3.cloned.1.call-done) | copy-start | bytes 25165828
  138.7 23.2 %copy-start.14 = (f32[64,1536]{1,0:T(8,128)S(1)}, f32[64,1536]{1,0:T(8,128)}, u32[]{:S(2)}) copy-start(f32[64,1536]{1,0:T(8,128)} %fitted_ref.1) | copy-start | bytes 1179652
  157.9 6.6 %collective-permute-start.4 = (f32[64,8,128]{2,1,0:T(8,128)S(1)}, f32[64,8,128]{2,1,0:T(8,128)S(1)}, u32[]{:S(2)}, u32[]{:S(2)}) collective-permute-start(f32[64,8,128]{2,1,0:T(8,128)S(1)} %all_to_all.29.delta_ref), channel_id=1, source_target_pairs={{0,4},{4,0},{1,5},{5,1},{2,6},{6,2},{3,7},{7,3},{8,12},{12,8},{9,1... | collective-permute-start | bytes 786440 | tf_op jit(solution)/shard_map/ppermute | solution.py:56
Sparse Core Ops, SparseCore 0:
  11.1 98.4 all-gather.2

commit v4 on v3

--- a/solution.py
+++ b/solution.py
@@ -12,15 +12,19 @@
 ZY = ("z", "y")
 DP = ("z", "y", "c")
 FEATURE_ROWS = 512
+KEPT_ROWS = 448
 LANES = 128
 CHUNK = 256
 UNIT = 768
+SHARE = 16
 VMEM_BYTES = 16 * 1024 * 1024
+BETWEEN_BYTES = 36 * 1024 * 1024
 BF16 = jnp.bfloat16
 F32 = jnp.float32
 TRANSPOSED = (((1,), (1,)), ((), ()))
 FIRST_DIMS = (((0,), (0,)), ((), ()))
 WHOLE = pl.BlockSpec(memory_space=pltpu.VMEM)
+FAR = pl.BlockSpec(memory_space=pltpu.HBM)
 
 
 def call(
@@ -29,20 +33,22 @@
     shapes,
     owners,
     *args,
+    in_specs=None,
     scratch=(),
     cost=None,
+    vmem=VMEM_BYTES,
 ):
     return pl.pallas_call(
         kernel,
         grid_spec=pltpu.PrefetchScalarGridSpec(
             num_scalar_prefetch=1,
             grid=(),
-            in_specs=[WHOLE] * len(args),
+            in_specs=in_specs or [WHOLE] * len(args),
             out_specs=[WHOLE] * len(shapes),
             scratch_shapes=list(scratch),
         ),
         out_shape=[jax.ShapeDtypeStruct(*shape) for shape in shapes],
-        compiler_params=pltpu.CompilerParams(vmem_limit_bytes=VMEM_BYTES),
+        compiler_params=pltpu.CompilerParams(vmem_limit_bytes=vmem),
         cost_estimate=cost,
         name=name,
     )(owners, *args)
@@ -153,7 +159,7 @@
     count = points_ref.shape[1]
     outs = weights_ref.shape[0]
     gamma = 2.0 / features
-    empty = jnp.zeros((FEATURE_ROWS - features, LANES), F32)
+    empty = jnp.zeros((KEPT_ROWS - features, LANES), F32)
     for at in range(0, count, LANES):
         rows = slice(at, at + LANES)
         wide = jnp.concatenate([points_ref[:, rows].astype(F32), empty], axis=0)
@@ -188,7 +194,7 @@
 
     blocks, block_norms, grads = [], [], []
     for step in range(steps):
-        rows = slice(step * FEATURE_ROWS, (step + 1) * FEATURE_ROWS)
+        rows = slice(step * KEPT_ROWS, (step + 1) * KEPT_ROWS)
         for pair in range(pairs):
             block = jnp.concatenate(
                 [blocks_ref[2 * pair, rows, :], blocks_ref[2 * pair + 1, rows, :]], axis=1
@@ -257,7 +263,7 @@
     kern = (tiles // 2, count, 2 * LANES)
     shapes = [((outs, tiles, LANES), F32), (kern, BF16), (kern, BF16)]
     if first:
-        shapes += [((count, FEATURE_ROWS), BF16), ((count, 1), F32), ((2 * outs, count), BF16)]
+        shapes += [((count, KEPT_ROWS), BF16), ((count, 1), F32), ((2 * outs, count), BF16)]
     return call(
         functools.partial(first_kernel if first else second_kernel, features),
         "first_half" if first else "second_half",
@@ -269,21 +275,29 @@
         index,
         blocks,
         cost=pl.CostEstimate(
-            flops=tiles * LANES * count * (2 * FEATURE_ROWS + 6 * outs),
+            flops=tiles * LANES * count * (2 * KEPT_ROWS + 6 * outs),
             bytes_accessed=4 * tiles * LANES * count,
             transcendentals=tiles * LANES * count,
         ),
     )
 
 
-def between_kernel(features, owners, index_ref, own_ref, other_ref, out_ref):
+def between_kernel(
+    features, owners, index_ref, own_ref, other_ref, given_far, out_ref, given_ref, sems
+):
+    copies = [
+        pltpu.make_async_copy(given_far.at[rows], given_ref.at[rows], sems.at[n])
+        for n, rows in enumerate(slice(at, at + SHARE) for at in range(0, given_ref.shape[0], SHARE))
+    ]
+    for copy in copies:
+        copy.start()
     lines = own_ref.shape[0]
     gamma = 2.0 / features
     core = lax.axis_index("c")
 
     def tile(step, line, kind):
-        at = step * FEATURE_ROWS
-        rows = slice(at, at + FEATURE_ROWS)
+        at = step * KEPT_ROWS
+        rows = slice(at, at + KEPT_ROWS)
         return jnp.where(core == kind, own_ref[line, rows, :], other_ref[line, rows, :])
 
     places = [(line, kind) for line in range(lines) for kind in range(2)]
@@ -307,24 +321,30 @@
         out_ref[n * LANES : (n + 1) * LANES, :] = kern + jnp.where(
             first_index == second_index, extra, 0.0
         )
-
-
-def between_blocks(features, owners, index, own, other):
+    for copy in copies:
+        copy.wait()
+
+
+def between_blocks(features, owners, index, own, other, given):
     block = index.shape[1]
     return call(
         functools.partial(between_kernel, features),
         "between_blocks",
-        [((block, block), F32)],
+        [((block, block), F32), (given.shape, F32)],
         owners,
         index,
         own,
         other,
+        given,
+        in_specs=[WHOLE] * 3 + [FAR],
+        scratch=[pltpu.SemaphoreType.DMA((given.shape[0] // SHARE,))],
         cost=pl.CostEstimate(
-            flops=2 * block * block * FEATURE_ROWS,
+            flops=2 * block * block * KEPT_ROWS,
             bytes_accessed=4 * block * block,
             transcendentals=block * block,
         ),
-    )[0]
+        vmem=BETWEEN_BYTES,
+    )
 
 
 def chain_kernel(owners, mine_ref, theirs_ref, given_ref, between_ref, out_ref, grads):
@@ -377,6 +397,17 @@
         between,
         scratch=[pltpu.VMEM((2, block), F32)],
     )[0]
+
+
+def total_kernel(owners, parts_ref, out_ref):
+    total = parts_ref[0]
+    for n in range(1, parts_ref.shape[0]):
+        total += parts_ref[n]
+    out_ref[...] = total
+
+
+def total(owners, parts):
+    return call(total_kernel, "total", [(parts.shape[1:], F32)], owners, parts)[0]
 
 
 def update_kernel(
@@ -462,7 +493,8 @@
     keep, send = pick_blocks(points.T, block_index)
     parcels = choose(owners, keep, exchange(send)).reshape(groups, -1, LANES)
     blocks = all_to_all(take(owners, all_to_all(parcels, ZY)), ZY)
-    blocks = blocks.reshape(1, steps * FEATURE_ROWS, LANES)
+    blocks = blocks.reshape(steps, FEATURE_ROWS, LANES)[:, :KEPT_ROWS]
+    blocks = blocks.reshape(1, steps * KEPT_ROWS, LANES)
     own = all_to_all(jnp.broadcast_to(blocks, (lines, *blocks.shape[1:])), "x")
     other = exchange(own)
 
@@ -476,9 +508,9 @@
     )
     grad = all_to_all(grad_other + grad_theirs, ZY)
     grad, given, own, other = lax.optimization_barrier((grad, given, own, other))
-    grad = jnp.sum(grad, axis=0)
+    grad = total(owners, grad)
     theirs = exchange(grad)
-    between = between_blocks(features, owners, block_index, own, other)
+    between, given = between_blocks(features, owners, block_index, own, other, given)
     mine = run_chain(owners, grad, theirs, given, between)
 
     mine = all_to_all(jnp.broadcast_to(mine, (groups, *mine.shape)), ZY)

time: 176 us -> 172 us (0.977)
  local copies, waits for them, and re-layouts: 14.5 us -> 10.8 us
  Pallas kernels: 22.2 us -> 25 us
    unnamed x42, local copies, waits for them, and re-layouts: 14.3 us -> 10.7 us
    pallas_call x8 -> x9, Pallas kernels: 21.4 us -> 24.1 us  [call(): pl.pallas_call(kernel, grid_spec=pltpu.PrefetchScalarGridSpec(num_scalar_...]
  transfers between devices with their start and end apart: 6 -> 6, of which waited for: 1 -> 1; matrix products, arithmetic and copies ran while one was open for 0% -> 0% of each run, Pallas kernels for 10% -> 11%
where the time goes in v4:
time: 172 us; the launch traced here: 171 us
  blocking collectives  93 us (54%)
  starting transfers between devices  26.3 us (15%)
  Pallas kernels  25 us (15%)
  between operations  14.4 us (8%)
  local copies, waits for them, and re-layouts  10.8 us (6%)
  waiting for transfers between devices  1.83 us (1%)
    all_to_all x5, blocking collectives, all_to_all(): return lax.all_to_all(value, axes, 0, 0, tiled=True)  93 us
    ppermute x5, starting transfers between devices, exchange(): return lax.ppermute(value, 'c', [(0, 1), (1, 0)])  26.3 us
    pallas_call x9, Pallas kernels, call(): pl.pallas_call(kernel, grid_spec=pltpu.PrefetchScalarGridSpec(num_scalar_...  24.1 us
    unnamed x42, local copies, waits for them, and re-layouts  10.7 us
  transfers between devices with their start and end apart: 6, of which 1 were waited for; matrix products, arithmetic and copies ran while one was open for 0% of the time, Pallas kernels for 11%

profile of v4, /device:TPU:1, one launch (start us, length us, event | category | flops | bytes accessed | tf_op | source)
XLA Modules:
  0.0 171.4 jit_solution(1024132367036542995)
XLA Ops:
  7.2 0.0 all-gather.3.cloned.1.call-start
  7.2 0.7 all-gather.3.cloned.1.call-update
  7.9 0.0 copy-start.8
  7.9 1.3 copy-done.8
  9.2 0.0 copy-start.15
  9.2 0.7 copy-done.15
  9.9 0.9 pick_blocks.1
  10.8 0.0 copy-start.9
  10.8 0.0 copy-start.12
  10.8 8.9 %collective-permute-start = (bf16[2,512,128]{2,1,0:T(8,128)(2,1)S(1)}, bf16[2,512,128]{2,1,0:T(8,128)(2,1)S(1)}, u32[]{:S(2)}, u32[]{:S(2)}) collective-permute-start(bf16[2,512,128]{2,1,0:T(8,128)(2,1)S(1)} %get-tuple-element.22), channel_id=1, source_target_pairs={{0,4},{4,0},{1,5},{5,1},{2,6},{6,2},{3,7},{7,3},{8,12},{12,8},{9,1... | collective-permute-start | bytes 786440 | tf_op jit(solution)/shard_map/ppermute | solution.py:62
  19.8 1.1 collective-permute-done.got_ref
  20.9 0.0 copy-start.17
  20.9 0.7 copy-done.17
  21.6 0.6 choose.1
  22.2 24.8 %all_to_all.25.parcels_ref = bf16[64,16,128]{2,1,0:T(8,128)(2,1)S(1)} all-to-all(bf16[64,16,128]{2,1,0:T(8,128)(2,1)S(1)} %bitcast.7), channel_id=1, replica_groups=mesh['z'=8,'y'=8,'c'=2,'x'=4] {'z','y'}, dimensions={0} | all-to-all | bytes 524288 | tf_op jit(solution)/shard_map/all_to_all | solution.py:66
  47.0 0.7 copy-done.18
  47.6 0.6 take.1
  48.2 17.6 %all_to_all.26 = bf16[64,16,128]{2,1,0:T(8,128)(2,1)S(1)} all-to-all(bf16[64,16,128]{2,1,0:T(8,128)(2,1)S(1)} %take.1), channel_id=1, replica_groups=mesh['z'=8,'y'=8,'c'=2,'x'=4] {'z','y'}, dimensions={0} | all-to-all | bytes 524288 | tf_op jit(solution)/shard_map/all_to_all | solution.py:66
  65.9 0.1 broadcast_in_dim.11
  66.0 13.8 %all_to_all.27.blocks.own_ref = bf16[4,896,128]{2,1,0:T(8,128)(2,1)S(1)} all-to-all(bf16[4,896,128]{2,1,0:T(8,128)(2,1)S(1)} %broadcast_in_dim.11), channel_id=1, replica_groups=mesh['z'=8,'y'=8,'c'=2,'x'=4] {'x'}, dimensions={0} | all-to-all | bytes 1835008 | tf_op jit(solution)/shard_map/all_to_all | solution.py:66
  79.8 6.7 %collective-permute-start.1 = (bf16[4,896,128]{2,1,0:T(8,128)(2,1)S(1)}, bf16[4,896,128]{2,1,0:T(8,128)(2,1)S(1)}, u32[]{:S(2)}, u32[]{:S(2)}) collective-permute-start(bf16[4,896,128]{2,1,0:T(8,128)(2,1)S(1)} %all_to_all.27.blocks.own_ref), channel_id=1, source_target_pairs={{0,4},{4,0},{1,5},{5,1},{2,6},{6,2},{3,7},{7,3},{8,12},{12,8},{9,1... | collective-permute-start | bytes 2752520 | tf_op jit(solution)/shard_map/ppermute | solution.py:62
  86.5 0.0 copy-done.20
  86.5 0.0 copy-done.9
  86.5 0.0 copy-done.12
  86.5 5.1 %first_half.1 = (f32[64,8,128]{2,1,0:T(8,128)S(1)}, bf16[4,1536,256]{2,1,0:T(8,128)(2,1)S(1)}, bf16[4,1536,256]{2,1,0:T(8,128)(2,1)S(1)}, bf16[1536,448]{1,0:T(8...) custom-call(s32[2]{0:T(128)S(1)} %copy-done.18, bf16[440,1536]{1,0:T(8,128)(2,1)S(1)} %bitcast.6, ...), custom_call_target="tpu_custom_call" | custom-call | flops 2013265920 | bytes 6291456 | tf_op jit(solution)/shard_map/first_half/pallas_call | solution.py:41
  91.6 0.0 copy-done.6
  91.6 0.0 copy-start
  91.7 1.6 copy-done
  93.3 1.9 %collective-permute-start.2 = (f32[64,8,128]{2,1,0:T(8,128)S(1)}, f32[64,8,128]{2,1,0:T(8,128)S(1)}, u32[]{:S(2)}, u32[]{:S(2)}) collective-permute-start(f32[64,8,128]{2,1,0:T(8,128)S(1)} %get-tuple-element.27), channel_id=1, source_target_pairs={{0,4},{4,0},{1,5},{5,1},{2,6},{6,2},{3,7},{7,3},{8,12},{12,8},{9,1... | collective-permute-start | bytes 786440 | tf_op jit(solution)/shard_map/ppermute | solution.py:62
  95.2 0.0 collective-permute-done.1.refs_7_.other_ref
  95.2 0.0 copy-start.10
  95.2 0.0 copy-done.16
  95.2 0.0 copy-start.19
  95.3 4.7 %second_half.1 = (f32[64,8,128]{2,1,0:T(8,128)S(1)}, bf16[4,1536,256]{2,1,0:T(8,128)(2,1)S(1)}, bf16[4,1536,256]{2,1,0:T(8,128)(2,1)S(1)}) custom-call(s32[2]{0:T(128)S(1)} %copy-done.18, bf16[1536,448]{1,0:T(8,128)(2,1)S(1)} %get-tuple-element.23.refs_1_, f32[1536,1]{1,0:T(8,128)S(1)} %get-tuple-element.24.refs_2_, ...), custom_call_target="tpu_custom_call" | custom-call | flops 2013265920 | bytes 6291456 | tf_op jit(solution)/shard_map/second_half/pallas_call | solution.py:41
  99.9 0.0 copy-done.10
  100.0 0.0 copy-start.2
  100.0 1.7 copy-done.2
  101.6 1.6 copy-done.4
  103.3 0.0 collective-permute-done.2
  103.3 19.0 %all_to_all.28.parts_ref = f32[64,8,128]{2,1,0:T(8,128)S(1)} all-to-all(f32[64,8,128]{2,1,0:T(8,128)S(1)} %add.3), channel_id=1, replica_groups=mesh['z'=8,'y'=8,'c'=2,'x'=4] {'z','y'}, dimensions={0} | all-to-all | bytes 524288 | tf_op jit(solution)/shard_map/all_to_all | solution.py:66
  122.3 0.0 copy-done.19
  122.3 0.6 total.1.mine_ref
  122.9 4.9 %collective-permute-start.3 = (f32[8,128]{1,0:T(8,128)S(1)}, f32[8,128]{1,0:T(8,128)S(1)}, u32[]{:S(2)}, u32[]{:S(2)}) collective-permute-start(f32[8,128]{1,0:T(8,128)S(1)} %total.1.mine_ref), channel_id=1, source_target_pairs={{0,4},{4,0},{1,5},{5,1},{2,6},{6,2},{3,7},{7,3},{8,12},{12,8},{9,1... | collective-permute-start | bytes 12296 | tf_op jit(solution)/shard_map/ppermute | solution.py:62
  127.8 0.0 copy-start.7
  127.8 1.2 copy-done.7
  129.0 1.2 copy-done.11
  130.2 4.8 %between_blocks.1 = (f32[1024,1024]{1,0:T(8,128)S(1)}, f32[128,2,8,1024]{3,2,1,0:T(8,128)S(1)}) custom-call(s32[2]{0:T(128)S(1)} %copy-done.19, s32[2,1024]{1,0:T(2,128)S(1)} %copy-done.16, bf16[4,896,128]{2,1,0:T(8,128)(2,1)S(1)} %copy-done.7, bf16[4,896,128]{2,1,0:T(8,128)(2,1)S(1)} %copy-done.11, f32[128,2,8,1024]{3,2,1,0:T(8,128)} %bitcast.8), custom_call_target="tpu_custom_call" | custom-call | flops 939524096 | bytes 4194304 | tf_op jit(solution)/shard_map/between_blocks/pallas_call | solution.py:41
  135.0 0.0 collective-permute-done.3.theirs_ref
  135.0 0.0 copy-start.1
  135.0 0.0 copy-start.3
  135.0 0.0 copy-start.5
  135.0 0.0 copy-start.13
  135.1 0.0 copy-start.14
  135.1 1.5 run_chain.1
  136.6 17.9 %all_to_all.29.delta_ref = f32[64,8,128]{2,1,0:T(8,128)S(1)} all-to-all(f32[64,8,128]{2,1,0:T(8,128)S(1)} %broadcast_in_dim.12), channel_id=1, replica_groups=mesh['z'=8,'y'=8,'c'=2,'x'=4] {'z','y'}, dimensions={0} | all-to-all | bytes 524288 | tf_op jit(solution)/shard_map/all_to_all | solution.py:66
  154.5 3.8 %collective-permute-start.4 = (f32[64,8,128]{2,1,0:T(8,128)S(1)}, f32[64,8,128]{2,1,0:T(8,128)S(1)}, u32[]{:S(2)}, u32[]{:S(2)}) collective-permute-start(f32[64,8,128]{2,1,0:T(8,128)S(1)} %all_to_all.29.delta_ref), channel_id=1, source_target_pairs={{0,4},{4,0},{1,5},{5,1},{2,6},{6,2},{3,7},{7,3},{8,12},{12,8},{9,1... | collective-permute-start | bytes 786440 | tf_op jit(solution)/shard_map/ppermute | solution.py:62
  158.3 0.0 copy-done.1
  158.4 0.0 copy-done.3
  158.4 0.0 copy-done.5
  158.4 0.0 copy-done.13
  158.4 0.0 copy-done.14
  158.4 2.6 %update.2 = (f32[64,1536]{1,0:T(8,128)S(1)}, f32[64,1536]{1,0:T(8,128)S(1)}) custom-call(s32[2]{0:T(128)S(1)} %copy-done.19, f32[64,8,128]{2,1,0:T(8,128)S(1)} %all_to_all.29.delta_ref, s32[2,1024]{1,0:T(2,128)S(1)} %copy-done.16, f32[64,1536]{1,0:T(8,128)S(1)} %copy-done.13, f32[64,1536]{1,0:T(8,128)S(1)} %copy-done.14, ...), custom_call_target="tpu_custom_call" | custom-call | flops 603979776 | bytes 6291456 | tf_op jit(solution)/shard_map/update/pallas_call | solution.py:41
  161.0 0.0 collective-permute-done.4.delta_ref
  161.0 3.5 %update.3 = (f32[64,1536]{1,0:T(8,128)}, f32[64,1536]{1,0:T(8,128)}) custom-call(s32[2]{0:T(128)S(1)} %copy-done.19, f32[64,8,128]{2,1,0:T(8,128)S(1)} %collective-permute-done.4.delta_ref, s32[2,1024]{1,0:T(2,128)S(1)} %copy-done.16, f32[64,1536]{1,0:T(8,128)S(1)} %get-tuple-element.38.weights_ref, f32[64,1536]{1,0:T(8,128)S(1)} %get-tuple-element.39.fitted_ref, ...), custom_call_target="tpu_custom_call" | custom-call | flops 603979776 | bytes 6291456 | tf_op jit(solution)/shard_map/update/pallas_call | solution.py:41
  (10 shorter events, 0.1 us)
Async XLA Ops:
  7.2 115.2 %all-gather.3.cloned.1.call-start = ((), (), s32[]{:S(2)}) async-start(), calls=%async_computation.5 | async-start | bytes 8454144 | tf_op jit(solution)/shard_map/all_gather | solution.py:491
  7.9 1.3 copy-start.8
  9.2 0.7 copy-start.15
  9.9 76.6 %copy-start.20 = (f32[64,1536]{1,0:T(8,128)S(1)}, f32[64,1536]{1,0:T(8,128)}, u32[]{:S(2)}) copy-start(f32[64,1536]{1,0:T(8,128)} %refs_5_.1) | copy-start | bytes 1179652
  10.8 75.7 %copy-start.9 = (bf16[1536,440]{0,1:T(8,128)(2,1)S(1)}, bf16[1536,440]{0,1:T(8,128)(2,1)}, u32[]{:S(2)}) copy-start(bf16[1536,440]{0,1:T(8,128)(2,1)} %param.7) | copy-start | bytes 4055044
  10.8 75.7 %copy-start.12 = (f32[64,1536]{1,0:T(8,128)S(1)}, f32[64,1536]{1,0:T(8,128)}, u32[]{:S(2)}) copy-start(f32[64,1536]{1,0:T(8,128)} %weights_ref.1) | copy-start | bytes 1179652
  10.8 10.1 %collective-permute-start = (bf16[2,512,128]{2,1,0:T(8,128)(2,1)S(1)}, bf16[2,512,128]{2,1,0:T(8,128)(2,1)S(1)}, u32[]{:S(2)}, u32[]{:S(2)}) collective-permute-start(bf16[2,512,128]{2,1,0:T(8,128)(2,1)S(1)} %get-tuple-element.22), channel_id=1, source_target_pairs={{0,4},{4,0},{1,5},{5,1},{2,6},{6,2},{3,7},{7,3},{8,12},{12,8},{9,1... | collective-permute-start | bytes 786440 | tf_op jit(solution)/shard_map/ppermute | solution.py:62
  20.9 0.7 copy-start.17
  47.0 0.7 copy-start.18
  79.7 11.9 %copy-start.6 = (bf16[4,896,128]{2,1,0:T(8,128)(2,1)}, bf16[4,896,128]{2,1,0:T(8,128)(2,1)S(1)}, u32[]{:S(2)}) copy-start(bf16[4,896,128]{2,1,0:T(8,128)(2,1)S(1)} %all_to_all.27.blocks.own_ref) | copy-start | bytes 2752516
  79.7 15.5 %copy-start.16 = (s32[2,1024]{1,0:T(2,128)S(1)}, s32[2,1024]{1,0:T(2,128)}, u32[]{:S(2)}) copy-start(s32[2,1024]{1,0:T(2,128)} %index_ref.7) | copy-start | bytes 24580
  79.8 15.5 %collective-permute-start.1 = (bf16[4,896,128]{2,1,0:T(8,128)(2,1)S(1)}, bf16[4,896,128]{2,1,0:T(8,128)(2,1)S(1)}, u32[]{:S(2)}, u32[]{:S(2)}) collective-permute-start(bf16[4,896,128]{2,1,0:T(8,128)(2,1)S(1)} %all_to_all.27.blocks.own_ref), channel_id=1, source_target_pairs={{0,4},{4,0},{1,5},{5,1},{2,6},{6,2},{3,7},{7,3},{8,12},{12,8},{9,1... | collective-permute-start | bytes 2752520 | tf_op jit(solution)/shard_map/ppermute | solution.py:62
  91.6 1.6 copy-start
  93.3 10.0 %collective-permute-start.2 = (f32[64,8,128]{2,1,0:T(8,128)S(1)}, f32[64,8,128]{2,1,0:T(8,128)S(1)}, u32[]{:S(2)}, u32[]{:S(2)}) collective-permute-start(f32[64,8,128]{2,1,0:T(8,128)S(1)} %get-tuple-element.27), channel_id=1, source_target_pairs={{0,4},{4,0},{1,5},{5,1},{2,6},{6,2},{3,7},{7,3},{8,12},{12,8},{9,1... | collective-permute-start | bytes 786440 | tf_op jit(solution)/shard_map/ppermute | solution.py:62
  95.2 4.7 %copy-start.10 = (bf16[4,896,128]{2,1,0:T(8,128)(2,1)}, bf16[4,896,128]{2,1,0:T(8,128)(2,1)S(1)}, u32[]{:S(2)}) copy-start(bf16[4,896,128]{2,1,0:T(8,128)(2,1)S(1)} %collective-permute-done.1.refs_7_.other_ref) | copy-start | bytes 2752516
  95.2 27.1 %copy-start.19 = (s32[2]{0:T(128)S(1)}, s32[2]{0:T(128)}, u32[]{:S(2)}) copy-start(s32[2]{0:T(128)} %owners.15) | copy-start | bytes 28
  100.0 1.7 copy-start.2
  101.6 1.6 copy-start.4
  122.9 12.1 %collective-permute-start.3 = (f32[8,128]{1,0:T(8,128)S(1)}, f32[8,128]{1,0:T(8,128)S(1)}, u32[]{:S(2)}, u32[]{:S(2)}) collective-permute-start(f32[8,128]{1,0:T(8,128)S(1)} %total.1.mine_ref), channel_id=1, source_target_pairs={{0,4},{4,0},{1,5},{5,1},{2,6},{6,2},{3,7},{7,3},{8,12},{12,8},{9,1... | collective-permute-start | bytes 12296 | tf_op jit(solution)/shard_map/ppermute | solution.py:62
  127.8 1.2 copy-start.7
  129.0 1.2 copy-start.11
  135.0 23.3 %copy-start.1 = (bf16[4,1536,256]{2,1,0:T(8,128)(2,1)S(1)}, bf16[4,1536,256]{2,1,0:T(8,128)(2,1)}, u32[]{:S(2)}) copy-start(bf16[4,1536,256]{2,1,0:T(8,128)(2,1)} %copy-done) | copy-start | bytes 9437188
  135.0 23.3 %copy-start.3 = (bf16[4,1536,256]{2,1,0:T(8,128)(2,1)S(1)}, bf16[4,1536,256]{2,1,0:T(8,128)(2,1)}, u32[]{:S(2)}) copy-start(bf16[4,1536,256]{2,1,0:T(8,128)(2,1)} %copy-done.2) | copy-start | bytes 9437188
  135.0 23.3 %copy-start.5 = (bf16[4,1536,256]{2,1,0:T(8,128)(2,1)S(1)}, bf16[4,1536,256]{2,1,0:T(8,128)(2,1)}, u32[]{:S(2)}) copy-start(bf16[4,1536,256]{2,1,0:T(8,128)(2,1)} %copy-done.4) | copy-start | bytes 9437188
  135.0 23.3 %copy-start.13 = (f32[64,1536]{1,0:T(8,128)S(1)}, f32[64,1536]{1,0:T(8,128)}, u32[]{:S(2)}) copy-start(f32[64,1536]{1,0:T(8,128)} %weights_ref.1) | copy-start | bytes 1179652
  135.1 23.3 %copy-start.14 = (f32[64,1536]{1,0:T(8,128)S(1)}, f32[64,1536]{1,0:T(8,128)}, u32[]{:S(2)}) copy-start(f32[64,1536]{1,0:T(8,128)} %fitted_ref.1) | copy-start | bytes 1179652
  154.5 6.5 %collective-permute-start.4 = (f32[64,8,128]{2,1,0:T(8,128)S(1)}, f32[64,8,128]{2,1,0:T(8,128)S(1)}, u32[]{:S(2)}, u32[]{:S(2)}) collective-permute-start(f32[64,8,128]{2,1,0:T(8,128)S(1)} %all_to_all.29.delta_ref), channel_id=1, source_target_pairs={{0,4},{4,0},{1,5},{5,1},{2,6},{6,2},{3,7},{7,3},{8,12},{12,8},{9,1... | collective-permute-start | bytes 786440 | tf_op jit(solution)/shard_map/ppermute | solution.py:62
Sparse Core Ops, SparseCore 0:
  11.1 98.4 all-gather.2

commit v5 on v4

--- a/solution.py
+++ b/solution.py
@@ -16,7 +16,7 @@
 LANES = 128
 CHUNK = 256
 UNIT = 768
-SHARE = 16
+SHARE = 32
 VMEM_BYTES = 16 * 1024 * 1024
 BETWEEN_BYTES = 36 * 1024 * 1024
 BF16 = jnp.bfloat16

time: 172 us -> 172 us (level)
  no operation moved by 1% of the time
where the time goes in v5:
time: 172 us; the launch traced here: 171 us
  blocking collectives  93 us (54%)
  starting transfers between devices  26.3 us (15%)
  Pallas kernels  25 us (15%)
  between operations  14.4 us (8%)
  local copies, waits for them, and re-layouts  10.8 us (6%)
  waiting for transfers between devices  1.83 us (1%)
    all_to_all x5, blocking collectives, all_to_all(): return lax.all_to_all(value, axes, 0, 0, tiled=True)  93 us
    ppermute x5, starting transfers between devices, exchange(): return lax.ppermute(value, 'c', [(0, 1), (1, 0)])  26.3 us
    pallas_call x9, Pallas kernels, call(): pl.pallas_call(kernel, grid_spec=pltpu.PrefetchScalarGridSpec(num_scalar_...  24.1 us
    unnamed x42, local copies, waits for them, and re-layouts  10.7 us
  transfers between devices with their start and end apart: 6, of which 1 were waited for; matrix products, arithmetic and copies ran while one was open for 0% of the time, Pallas kernels for 11%

profile of v5, /device:TPU:1, one launch (start us, length us, event | category | flops | bytes accessed | tf_op | source)
XLA Modules:
  0.0 171.4 jit_solution(57681658223283905)
XLA Ops:
  7.2 0.0 all-gather.3.cloned.1.call-start
  7.2 0.7 all-gather.3.cloned.1.call-update
  7.9 0.0 copy-start.8
  7.9 1.3 copy-done.8
  9.2 0.0 copy-start.15
  9.2 0.7 copy-done.15
  9.9 0.0 copy-start.20
  9.9 0.9 pick_blocks.1
  10.8 0.0 copy-start.9
  10.8 0.0 copy-start.12
  10.8 8.9 %collective-permute-start = (bf16[2,512,128]{2,1,0:T(8,128)(2,1)S(1)}, bf16[2,512,128]{2,1,0:T(8,128)(2,1)S(1)}, u32[]{:S(2)}, u32[]{:S(2)}) collective-permute-start(bf16[2,512,128]{2,1,0:T(8,128)(2,1)S(1)} %get-tuple-element.22), channel_id=1, source_target_pairs={{0,4},{4,0},{1,5},{5,1},{2,6},{6,2},{3,7},{7,3},{8,12},{12,8},{9,1... | collective-permute-start | bytes 786440 | tf_op jit(solution)/shard_map/ppermute | solution.py:62
  19.8 1.1 collective-permute-done.got_ref
  20.9 0.7 copy-done.17
  21.6 0.6 choose.1
  22.2 24.8 %all_to_all.25.parcels_ref = bf16[64,16,128]{2,1,0:T(8,128)(2,1)S(1)} all-to-all(bf16[64,16,128]{2,1,0:T(8,128)(2,1)S(1)} %bitcast.7), channel_id=1, replica_groups=mesh['z'=8,'y'=8,'c'=2,'x'=4] {'z','y'}, dimensions={0} | all-to-all | bytes 524288 | tf_op jit(solution)/shard_map/all_to_all | solution.py:66
  47.0 0.7 copy-done.18
  47.6 0.6 take.1
  48.2 17.6 %all_to_all.26 = bf16[64,16,128]{2,1,0:T(8,128)(2,1)S(1)} all-to-all(bf16[64,16,128]{2,1,0:T(8,128)(2,1)S(1)} %take.1), channel_id=1, replica_groups=mesh['z'=8,'y'=8,'c'=2,'x'=4] {'z','y'}, dimensions={0} | all-to-all | bytes 524288 | tf_op jit(solution)/shard_map/all_to_all | solution.py:66
  65.9 0.1 broadcast_in_dim.11
  66.0 13.8 %all_to_all.27.blocks.own_ref = bf16[4,896,128]{2,1,0:T(8,128)(2,1)S(1)} all-to-all(bf16[4,896,128]{2,1,0:T(8,128)(2,1)S(1)} %broadcast_in_dim.11), channel_id=1, replica_groups=mesh['z'=8,'y'=8,'c'=2,'x'=4] {'x'}, dimensions={0} | all-to-all | bytes 1835008 | tf_op jit(solution)/shard_map/all_to_all | solution.py:66
  79.8 6.7 %collective-permute-start.1 = (bf16[4,896,128]{2,1,0:T(8,128)(2,1)S(1)}, bf16[4,896,128]{2,1,0:T(8,128)(2,1)S(1)}, u32[]{:S(2)}, u32[]{:S(2)}) collective-permute-start(bf16[4,896,128]{2,1,0:T(8,128)(2,1)S(1)} %all_to_all.27.blocks.own_ref), channel_id=1, source_target_pairs={{0,4},{4,0},{1,5},{5,1},{2,6},{6,2},{3,7},{7,3},{8,12},{12,8},{9,1... | collective-permute-start | bytes 2752520 | tf_op jit(solution)/shard_map/ppermute | solution.py:62
  86.5 0.0 copy-done.20
  86.5 0.0 copy-done.9
  86.5 0.0 copy-done.12
  86.5 5.1 %first_half.1 = (f32[64,8,128]{2,1,0:T(8,128)S(1)}, bf16[4,1536,256]{2,1,0:T(8,128)(2,1)S(1)}, bf16[4,1536,256]{2,1,0:T(8,128)(2,1)S(1)}, bf16[1536,448]{1,0:T(8...) custom-call(s32[2]{0:T(128)S(1)} %copy-done.18, bf16[440,1536]{1,0:T(8,128)(2,1)S(1)} %bitcast.6, ...), custom_call_target="tpu_custom_call" | custom-call | flops 2013265920 | bytes 6291456 | tf_op jit(solution)/shard_map/first_half/pallas_call | solution.py:41
  91.6 0.0 copy-done.6
  91.6 0.0 copy-start
  91.7 1.6 copy-done
  93.3 1.9 %collective-permute-start.2 = (f32[64,8,128]{2,1,0:T(8,128)S(1)}, f32[64,8,128]{2,1,0:T(8,128)S(1)}, u32[]{:S(2)}, u32[]{:S(2)}) collective-permute-start(f32[64,8,128]{2,1,0:T(8,128)S(1)} %get-tuple-element.27), channel_id=1, source_target_pairs={{0,4},{4,0},{1,5},{5,1},{2,6},{6,2},{3,7},{7,3},{8,12},{12,8},{9,1... | collective-permute-start | bytes 786440 | tf_op jit(solution)/shard_map/ppermute | solution.py:62
  95.2 0.0 collective-permute-done.1.refs_7_.other_ref
  95.2 0.0 copy-start.10
  95.2 0.0 copy-done.16
  95.2 0.0 copy-start.19
  95.3 4.7 %second_half.1 = (f32[64,8,128]{2,1,0:T(8,128)S(1)}, bf16[4,1536,256]{2,1,0:T(8,128)(2,1)S(1)}, bf16[4,1536,256]{2,1,0:T(8,128)(2,1)S(1)}) custom-call(s32[2]{0:T(128)S(1)} %copy-done.18, bf16[1536,448]{1,0:T(8,128)(2,1)S(1)} %get-tuple-element.23.refs_1_, f32[1536,1]{1,0:T(8,128)S(1)} %get-tuple-element.24.refs_2_, ...), custom_call_target="tpu_custom_call" | custom-call | flops 2013265920 | bytes 6291456 | tf_op jit(solution)/shard_map/second_half/pallas_call | solution.py:41
  99.9 0.0 copy-done.10
  100.0 0.0 copy-start.2
  100.0 1.7 copy-done.2
  101.6 1.6 copy-done.4
  103.3 0.0 collective-permute-done.2
  103.3 19.0 %all_to_all.28.parts_ref = f32[64,8,128]{2,1,0:T(8,128)S(1)} all-to-all(f32[64,8,128]{2,1,0:T(8,128)S(1)} %add.3), channel_id=1, replica_groups=mesh['z'=8,'y'=8,'c'=2,'x'=4] {'z','y'}, dimensions={0} | all-to-all | bytes 524288 | tf_op jit(solution)/shard_map/all_to_all | solution.py:66
  122.3 0.0 copy-done.19
  122.3 0.6 total.1.mine_ref
  122.9 4.9 %collective-permute-start.3 = (f32[8,128]{1,0:T(8,128)S(1)}, f32[8,128]{1,0:T(8,128)S(1)}, u32[]{:S(2)}, u32[]{:S(2)}) collective-permute-start(f32[8,128]{1,0:T(8,128)S(1)} %total.1.mine_ref), channel_id=1, source_target_pairs={{0,4},{4,0},{1,5},{5,1},{2,6},{6,2},{3,7},{7,3},{8,12},{12,8},{9,1... | collective-permute-start | bytes 12296 | tf_op jit(solution)/shard_map/ppermute | solution.py:62
  127.8 0.0 copy-start.7
  127.8 1.2 copy-done.7
  129.0 1.2 copy-done.11
  130.2 4.9 %between_blocks.1 = (f32[1024,1024]{1,0:T(8,128)S(1)}, f32[128,2,8,1024]{3,2,1,0:T(8,128)S(1)}) custom-call(s32[2]{0:T(128)S(1)} %copy-done.19, s32[2,1024]{1,0:T(2,128)S(1)} %copy-done.16, bf16[4,896,128]{2,1,0:T(8,128)(2,1)S(1)} %copy-done.7, bf16[4,896,128]{2,1,0:T(8,128)(2,1)S(1)} %copy-done.11, f32[128,2,8,1024]{3,2,1,0:T(8,128)} %bitcast.8), custom_call_target="tpu_custom_call" | custom-call | flops 939524096 | bytes 4194304 | tf_op jit(solution)/shard_map/between_blocks/pallas_call | solution.py:41
  135.0 0.0 collective-permute-done.3.theirs_ref
  135.0 0.0 copy-start.1
  135.0 0.0 copy-start.3
  135.1 0.0 copy-start.5
  135.1 0.0 copy-start.13
  135.1 0.0 copy-start.14
  135.1 1.5 run_chain.1
  136.7 17.9 %all_to_all.29.delta_ref = f32[64,8,128]{2,1,0:T(8,128)S(1)} all-to-all(f32[64,8,128]{2,1,0:T(8,128)S(1)} %broadcast_in_dim.12), channel_id=1, replica_groups=mesh['z'=8,'y'=8,'c'=2,'x'=4] {'z','y'}, dimensions={0} | all-to-all | bytes 524288 | tf_op jit(solution)/shard_map/all_to_all | solution.py:66
  154.5 3.8 %collective-permute-start.4 = (f32[64,8,128]{2,1,0:T(8,128)S(1)}, f32[64,8,128]{2,1,0:T(8,128)S(1)}, u32[]{:S(2)}, u32[]{:S(2)}) collective-permute-start(f32[64,8,128]{2,1,0:T(8,128)S(1)} %all_to_all.29.delta_ref), channel_id=1, source_target_pairs={{0,4},{4,0},{1,5},{5,1},{2,6},{6,2},{3,7},{7,3},{8,12},{12,8},{9,1... | collective-permute-start | bytes 786440 | tf_op jit(solution)/shard_map/ppermute | solution.py:62
  158.4 0.0 copy-done.1
  158.4 0.0 copy-done.3
  158.4 0.0 copy-done.5
  158.4 0.0 copy-done.13
  158.4 0.0 copy-done.14
  158.4 2.6 %update.2 = (f32[64,1536]{1,0:T(8,128)S(1)}, f32[64,1536]{1,0:T(8,128)S(1)}) custom-call(s32[2]{0:T(128)S(1)} %copy-done.19, f32[64,8,128]{2,1,0:T(8,128)S(1)} %all_to_all.29.delta_ref, s32[2,1024]{1,0:T(2,128)S(1)} %copy-done.16, f32[64,1536]{1,0:T(8,128)S(1)} %copy-done.13, f32[64,1536]{1,0:T(8,128)S(1)} %copy-done.14, ...), custom_call_target="tpu_custom_call" | custom-call | flops 603979776 | bytes 6291456 | tf_op jit(solution)/shard_map/update/pallas_call | solution.py:41
  161.0 0.0 collective-permute-done.4.delta_ref
  161.0 3.5 %update.3 = (f32[64,1536]{1,0:T(8,128)}, f32[64,1536]{1,0:T(8,128)}) custom-call(s32[2]{0:T(128)S(1)} %copy-done.19, f32[64,8,128]{2,1,0:T(8,128)S(1)} %collective-permute-done.4.delta_ref, s32[2,1024]{1,0:T(2,128)S(1)} %copy-done.16, f32[64,1536]{1,0:T(8,128)S(1)} %get-tuple-element.38.weights_ref, f32[64,1536]{1,0:T(8,128)S(1)} %get-tuple-element.39.fitted_ref, ...), custom_call_target="tpu_custom_call" | custom-call | flops 603979776 | bytes 6291456 | tf_op jit(solution)/shard_map/update/pallas_call | solution.py:41
  (10 shorter events, 0.1 us)
Async XLA Ops:
  7.2 115.2 %all-gather.3.cloned.1.call-start = ((), (), s32[]{:S(2)}) async-start(), calls=%async_computation.5 | async-start | bytes 8454144 | tf_op jit(solution)/shard_map/all_gather | solution.py:491
  7.9 1.3 copy-start.8
  9.2 0.7 copy-start.15
  9.9 76.6 %copy-start.20 = (f32[64,1536]{1,0:T(8,128)S(1)}, f32[64,1536]{1,0:T(8,128)}, u32[]{:S(2)}) copy-start(f32[64,1536]{1,0:T(8,128)} %refs_5_.1) | copy-start | bytes 1179652
  10.8 75.7 %copy-start.9 = (bf16[1536,440]{0,1:T(8,128)(2,1)S(1)}, bf16[1536,440]{0,1:T(8,128)(2,1)}, u32[]{:S(2)}) copy-start(bf16[1536,440]{0,1:T(8,128)(2,1)} %param.7) | copy-start | bytes 4055044
  10.8 75.7 %copy-start.12 = (f32[64,1536]{1,0:T(8,128)S(1)}, f32[64,1536]{1,0:T(8,128)}, u32[]{:S(2)}) copy-start(f32[64,1536]{1,0:T(8,128)} %weights_ref.1) | copy-start | bytes 1179652
  10.8 10.1 %collective-permute-start = (bf16[2,512,128]{2,1,0:T(8,128)(2,1)S(1)}, bf16[2,512,128]{2,1,0:T(8,128)(2,1)S(1)}, u32[]{:S(2)}, u32[]{:S(2)}) collective-permute-start(bf16[2,512,128]{2,1,0:T(8,128)(2,1)S(1)} %get-tuple-element.22), channel_id=1, source_target_pairs={{0,4},{4,0},{1,5},{5,1},{2,6},{6,2},{3,7},{7,3},{8,12},{12,8},{9,1... | collective-permute-start | bytes 786440 | tf_op jit(solution)/shard_map/ppermute | solution.py:62
  20.9 0.7 copy-start.17
  47.0 0.7 copy-start.18
  79.7 11.9 %copy-start.6 = (bf16[4,896,128]{2,1,0:T(8,128)(2,1)}, bf16[4,896,128]{2,1,0:T(8,128)(2,1)S(1)}, u32[]{:S(2)}) copy-start(bf16[4,896,128]{2,1,0:T(8,128)(2,1)S(1)} %all_to_all.27.blocks.own_ref) | copy-start | bytes 2752516
  79.7 15.5 %copy-start.16 = (s32[2,1024]{1,0:T(2,128)S(1)}, s32[2,1024]{1,0:T(2,128)}, u32[]{:S(2)}) copy-start(s32[2,1024]{1,0:T(2,128)} %index_ref.7) | copy-start | bytes 24580
  79.8 15.5 %collective-permute-start.1 = (bf16[4,896,128]{2,1,0:T(8,128)(2,1)S(1)}, bf16[4,896,128]{2,1,0:T(8,128)(2,1)S(1)}, u32[]{:S(2)}, u32[]{:S(2)}) collective-permute-start(bf16[4,896,128]{2,1,0:T(8,128)(2,1)S(1)} %all_to_all.27.blocks.own_ref), channel_id=1, source_target_pairs={{0,4},{4,0},{1,5},{5,1},{2,6},{6,2},{3,7},{7,3},{8,12},{12,8},{9,1... | collective-permute-start | bytes 2752520 | tf_op jit(solution)/shard_map/ppermute | solution.py:62
  91.6 1.6 copy-start
  93.3 10.0 %collective-permute-start.2 = (f32[64,8,128]{2,1,0:T(8,128)S(1)}, f32[64,8,128]{2,1,0:T(8,128)S(1)}, u32[]{:S(2)}, u32[]{:S(2)}) collective-permute-start(f32[64,8,128]{2,1,0:T(8,128)S(1)} %get-tuple-element.27), channel_id=1, source_target_pairs={{0,4},{4,0},{1,5},{5,1},{2,6},{6,2},{3,7},{7,3},{8,12},{12,8},{9,1... | collective-permute-start | bytes 786440 | tf_op jit(solution)/shard_map/ppermute | solution.py:62
  95.2 4.7 %copy-start.10 = (bf16[4,896,128]{2,1,0:T(8,128)(2,1)}, bf16[4,896,128]{2,1,0:T(8,128)(2,1)S(1)}, u32[]{:S(2)}) copy-start(bf16[4,896,128]{2,1,0:T(8,128)(2,1)S(1)} %collective-permute-done.1.refs_7_.other_ref) | copy-start | bytes 2752516
  95.2 27.1 %copy-start.19 = (s32[2]{0:T(128)S(1)}, s32[2]{0:T(128)}, u32[]{:S(2)}) copy-start(s32[2]{0:T(128)} %owners.15) | copy-start | bytes 28
  100.0 1.7 copy-start.2
  101.6 1.6 copy-start.4
  122.9 12.1 %collective-permute-start.3 = (f32[8,128]{1,0:T(8,128)S(1)}, f32[8,128]{1,0:T(8,128)S(1)}, u32[]{:S(2)}, u32[]{:S(2)}) collective-permute-start(f32[8,128]{1,0:T(8,128)S(1)} %total.1.mine_ref), channel_id=1, source_target_pairs={{0,4},{4,0},{1,5},{5,1},{2,6},{6,2},{3,7},{7,3},{8,12},{12,8},{9,1... | collective-permute-start | bytes 12296 | tf_op jit(solution)/shard_map/ppermute | solution.py:62
  127.8 1.2 copy-start.7
  129.0 1.2 copy-start.11
  135.0 23.3 %copy-start.1 = (bf16[4,1536,256]{2,1,0:T(8,128)(2,1)S(1)}, bf16[4,1536,256]{2,1,0:T(8,128)(2,1)}, u32[]{:S(2)}) copy-start(bf16[4,1536,256]{2,1,0:T(8,128)(2,1)} %copy-done) | copy-start | bytes 9437188
  135.0 23.3 %copy-start.3 = (bf16[4,1536,256]{2,1,0:T(8,128)(2,1)S(1)}, bf16[4,1536,256]{2,1,0:T(8,128)(2,1)}, u32[]{:S(2)}) copy-start(bf16[4,1536,256]{2,1,0:T(8,128)(2,1)} %copy-done.2) | copy-start | bytes 9437188
  135.1 23.3 %copy-start.5 = (bf16[4,1536,256]{2,1,0:T(8,128)(2,1)S(1)}, bf16[4,1536,256]{2,1,0:T(8,128)(2,1)}, u32[]{:S(2)}) copy-start(bf16[4,1536,256]{2,1,0:T(8,128)(2,1)} %copy-done.4) | copy-start | bytes 9437188
  135.1 23.3 %copy-start.13 = (f32[64,1536]{1,0:T(8,128)S(1)}, f32[64,1536]{1,0:T(8,128)}, u32[]{:S(2)}) copy-start(f32[64,1536]{1,0:T(8,128)} %weights_ref.1) | copy-start | bytes 1179652
  135.1 23.3 %copy-start.14 = (f32[64,1536]{1,0:T(8,128)S(1)}, f32[64,1536]{1,0:T(8,128)}, u32[]{:S(2)}) copy-start(f32[64,1536]{1,0:T(8,128)} %fitted_ref.1) | copy-start | bytes 1179652
  154.5 6.5 %collective-permute-start.4 = (f32[64,8,128]{2,1,0:T(8,128)S(1)}, f32[64,8,128]{2,1,0:T(8,128)S(1)}, u32[]{:S(2)}, u32[]{:S(2)}) collective-permute-start(f32[64,8,128]{2,1,0:T(8,128)S(1)} %all_to_all.29.delta_ref), channel_id=1, source_target_pairs={{0,4},{4,0},{1,5},{5,1},{2,6},{6,2},{3,7},{7,3},{8,12},{12,8},{9,1... | collective-permute-start | bytes 786440 | tf_op jit(solution)/shard_map/ppermute | solution.py:62
Sparse Core Ops, SparseCore 0:
  11.1 98.4 all-gather.2
